TPU v7x, 512 devices: a whole 4x4x16 slice. The times are simulated.
512 devices in a mesh: gy: 32 (over z_lo, y, core), gx: 16 (over x, z_hi).
Axes of the slice: x: 4, y: 4, z: 16 (z_hi: 4, z_lo: 4; z = z_hi * 4 + z_lo), core: 2. Of those that a mesh axis runs over, the one named last changes fastest.
Arguments:
- field: float32 [16, 2048, 2048], P(None, 'gy', 'gx'), may hold values from 0 to 1, as said below
- targets: float32 [3, 16], replicated, may hold values from 0.1 to 0.45
- weights: float32 [3, 16], replicated, may hold values from 0.3 to 3
Outputs:
- gradient: float32 [16, 2048, 2048], P(None, 'gy', 'gx')
- correlation: float32 [3, 16], replicated
Inputs may be any that keep to these rules, and one draw needn't show every extreme that they name: `field`: every value lies strictly between 0 and 1.
All inputs are finite; a program needn't handle non-finite values.
Results may differ from a plain program's by a relative error of at most 0.00028.
Values sent between devices are 32-bit elements; how exact they have to be, the bound alone decides.
No kernel may reach another device: no remote copies, remote signals or barrier semaphores. Data moves between devices by JAX's collectives and lax.ppermute only.
A program may use at most 128 MiB of HBM per device.

v0:
```python
import jax
import jax.numpy as jnp
from jax import lax
from jax.sharding import PartitionSpec as P

OFFSETS = 16


def with_halo(block, sides, width):
    for axis, dim in sides:
        count = lax.axis_size(axis)
        forward = [(i, i + 1) for i in range(count - 1)]
        forward.append((count - 1, 0))
        backward = [(target, source) for source, target in forward]
        low = lax.ppermute(
            lax.slice_in_dim(block, block.shape[dim] - width, None, axis=dim), axis, forward
        )
        high = lax.ppermute(lax.slice_in_dim(block, 0, width, axis=dim), axis, backward)
        block = jnp.concatenate([low, block, high], axis=dim)
    return block


def plane_shift(field, by):
    planes = field.shape[0]
    zeros = jnp.zeros((abs(by),) + field.shape[1:], jnp.float32)
    if by > 0:
        return jnp.concatenate([field[by:], zeros], axis=0)
    if by < 0:
        return jnp.concatenate([zeros, field[: planes + by]], axis=0)
    return field


def on_device(field, targets, weights):
    planes, rows, cols = field.shape
    width = OFFSETS - 1
    voxels = planes * rows * cols * lax.axis_size("gy") * lax.axis_size("gx")
    padded = with_halo(field, (("gy", 1), ("gx", 2)), width)
    along_rows = padded[:, :, width : width + cols]
    along_cols = padded[:, width : width + rows, :]
    plane_terms = []
    row_terms = []
    col_terms = []
    for step in range(OFFSETS):
        plane_terms.append(jnp.sum(field * plane_shift(field, step)))
        row_terms.append(jnp.sum(field * along_rows[:, width + step : width + step + rows, :]))
        col_terms.append(jnp.sum(field * along_cols[:, :, width + step : width + step + cols]))
    partial_sums = jnp.stack([jnp.stack(plane_terms), jnp.stack(row_terms), jnp.stack(col_terms)])
    totals = lax.psum(partial_sums, ("gy", "gx"))
    correlation = totals / jnp.float32(voxels)
    coefficient = weights * (correlation - targets)
    gradient = jnp.zeros_like(field)
    for step in range(OFFSETS):
        gradient = gradient + coefficient[0, step] * (
            plane_shift(field, step) + plane_shift(field, -step)
        )
    for step in range(OFFSETS):
        forward_rows = along_rows[:, width + step : width + step + rows, :]
        backward_rows = along_rows[:, width - step : width - step + rows, :]
        forward_cols = along_cols[:, :, width + step : width + step + cols]
        backward_cols = along_cols[:, :, width - step : width - step + cols]
        gradient = gradient + coefficient[1, step] * (forward_rows + backward_rows)
        gradient = gradient + coefficient[2, step] * (forward_cols + backward_cols)
    return (gradient, correlation)


def solution(mesh):
    return jax.shard_map(
        on_device,
        mesh=mesh,
        in_specs=(P(None, "gy", "gx"), P(), P()),
        out_specs=(P(None, "gy", "gx"), P()),
        check_vma=False,
    )
```

profile of v0, /device:TPU:1, one launch (start us, length us, event | category | flops | bytes accessed | tf_op | source)
XLA Modules:
  0.0 276.6 jit_solution(11242771562840031575)
XLA Ops:
  1.7 8.8 %collective-permute-start = (f32[16,15,128]{2,0,1:T(8,128)S(1)}, f32[16,15,128]{2,0,1:T(8,128)S(1)}, u32[]{:S(2)}, u32[]{:S(2)}) collective-permute-start(f32[16,15,128]{2,0,1:T(8,128)S(1)} %copy.175), channel_id=1, source_target_pairs={{16,0},{32,16},{48,32},{64,48},{80,64},{96,80},{112,96},{128,112},... | collective-permute-start | bytes 368648 | tf_op jit(solution)/shard_map/ppermute | solution.py:18
  10.6 1.9 collective-permute-start.1
  16.2 1.1 fusion.120
  20.5 1.5 fusion.118
  22.0 1.1 fusion.117
  23.1 1.3 fusion.116
  24.4 1.2 fusion.115
  25.6 1.3 fusion.114
  26.9 1.3 fusion.113
  28.2 1.3 fusion.112
  29.6 1.7 multiply_reduce_fusion.30
  32.5 5.7 %fusion.104 = (f32[]{:T(128)}, f32[]{:T(128)}, f32[]{:T(128)}, f32[]{:T(128)}, f32[]{:T(128)}, /*index=5*/f32[]{:T(128)}, f32[]{:T(128)}, f32[]{:T(128)}, f32[]{:T(128)}) fusion(f32[16,64,128]{1,0,2:T(8,128)S(1)} %copy.89, f32[16,15,128]{1,0,2:T(8,128)S(1)} %copy.120), kind=kLoop, calls=%fused_computation.161 | loop fusion | flops 3538935 | bytes 647204 | tf_op jit(solution)/shard_map/reduce_sum | solution.py:45
  38.2 1.4 copy.137
  40.8 10.6 %collective-permute-start.2 = (f32[16,94,15]{1,0,2:T(8,128)}, f32[16,94,15]{1,0,2:T(8,128)S(1)}, u32[]{:S(2)}, u32[]{:S(2)}) collective-permute-start(f32[16,94,15]{1,0,2:T(8,128)} %get-tuple-element.55), channel_id=1, source_target_pairs={{1,0},{2,1},{3,2},{4,3},{5,4},{6,5},{7,6},{8,7},{9,8},{10,9},{11,1... | collective-permute-start | bytes 270728 | tf_op jit(solution)/shard_map/ppermute | solution.py:18
  51.4 2.1 collective-permute-start.3
  53.5 4.1 %multiply_reduce_fusion.23 = (f32[]{:T(128)}, f32[]{:T(128)}, f32[]{:T(128)}, f32[]{:T(128)}, f32[]{:T(128)}, /*index=5*/f32[]{:T(128)}, f32[]{:T(128)}, f32[]{:...) fusion(f32[16,64,128]{1,0,2:T(8,128)S(1)} %copy.89, f32[16,15,128]{1,0,2:T(8,128)S(1)} %copy.120, ...), kind=kLoop, calls=%fused_computation.207 | loop fusion | flops 3932148 | bytes 1925168 | tf_op jit(solution)/shard_map/reduce_sum | solution.py:45
  57.7 9.9 %stack.194 = f32[16]{0:T(128)S(1)} concatenate(f32[1]{0:T(128)} %bitcast, f32[1]{0:T(128)} %bitcast.17, f32[1]{0:T(128)} %bitcast.18, f32[1]{0:T(128)} %bitcast.19, f32[1]{0:T(128)} %bitcast.20, f32[1]{0:T(128)} %bitcast.21, f32[1]{0:T(128)} %bitcast.22, f32[1]{0:T(128)} %bitcast.23, f32[1]{0:T(128)} %bitcast.24, f32[1]{0:T(128)} %bitcast.25, f32[1]{0:T(128)} %bitcast.26, ...), dimensions={0} | concatenate | bytes 128 | tf_op jit(solution)/shard_map/stack | solution.py:47
  68.7 3.4 %pad_maximum_fusion = (f32[16,94,143]{1,0,2:T(8,128)S(1)}, f32[16,94,143]{1,0,2:T(8,128)S(1)}) fusion(f32[16,94,15]{1,0,2:T(8,128)} %copy-done.17, f32[16,15,128]{1,0,2:T(8,128)} %copy-done, f32[16,64,128]{1,0,2:T(8,128)S(1)} %copy.89, f32[16,15,128]{1,0,2:T(8,128)} %copy-done.1, f32[16,94,15]{1,0,2:T(8,128)} %collective-permute-done.3), kind=kLoop, calls=%fused_computation.16 | loop fusion | flops 1290432 | bytes 2671104 | tf_op jit(solution)/shard_map/concatenate | solution.py:19
  72.2 5.1 %multiply_reduce_fusion = (f32[]{:T(128)}, f32[]{:T(128)}, f32[]{:T(128)}, f32[]{:T(128)}, f32[]{:T(128)}, /*index=5*/f32[]{:T(128)}, f32[]{:T(128)}, f32[]{:T(1...) fusion(f32[16,64,128]{1,0,2:T(8,128)S(1)} %copy.89, ...), kind=kLoop, calls=%fused_computation.184 | loop fusion | flops 4718574 | bytes 8585288 | tf_op jit(solution)/shard_map/reduce_sum | solution.py:46
  77.3 10.0 %stack.211 = f32[16]{0:T(128)S(1)} concatenate(f32[1]{0:T(128)} %bitcast, f32[1]{0:T(128)} %bitcast.33, f32[1]{0:T(128)} %bitcast.34, f32[1]{0:T(128)} %bitcast.35, f32[1]{0:T(128)} %bitcast.36, f32[1]{0:T(128)} %bitcast.37, f32[1]{0:T(128)} %bitcast.38, f32[1]{0:T(128)} %bitcast.39, f32[1]{0:T(128)} %bitcast.40, f32[1]{0:T(128)} %bitcast.41, f32[1]{0:T(128)} %bitcast.42, ...), dimensions={0} | concatenate | bytes 128 | tf_op jit(solution)/shard_map/stack | solution.py:47
  87.3 10.2 %stack.177 = f32[16]{0:T(128)S(1)} concatenate(f32[1]{0:T(128)} %bitcast, f32[1]{0:T(128)} %bitcast.1, f32[1]{0:T(128)} %bitcast.2, f32[1]{0:T(128)} %bitcast.3, f32[1]{0:T(128)} %bitcast.4, f32[1]{0:T(128)} %bitcast.5, f32[1]{0:T(128)} %bitcast.6, f32[1]{0:T(128)} %bitcast.7, f32[1]{0:T(128)} %bitcast.8, f32[1]{0:T(128)} %bitcast.9, f32[1]{0:T(128)} %bitcast.10, f32[1]{0:T(128)} %bitcast.11, ...), dimensions={0} | concatenate | bytes 128 | tf_op jit(solution)/shard_map/stack | solution.py:47
  97.5 108.5 %psum.7 = f32[3,16]{1,0:T(4,128)S(1)} all-reduce(f32[3,16]{1,0:T(4,128)S(1)} %pad_maximum_fusion.6), channel_id=1, replica_groups=mesh['gy'=32,'gx'=16] {'gy','gx'}, use_global_device_ids=true, to_apply=%region_46.0 | all-reduce | flops 48 | bytes 384 | tf_op jit(solution)/shard_map/psum | solution.py:48
  208.7 65.6 %fusion.40 = f32[16,64,128]{1,0,2:T(8,128)} fusion(f32[16,94,143]{1,0,2:T(8,128)S(1)} %get-tuple-element.54, f32[16,64,128]{1,0,2:T(8,128)S(1)} %copy.89, f32[16,15,128]{1,0,2:T(8,128)} %copy-done.1, f32[1,64,128]{1,0,2:T(1,128)} %get-tuple-element.86, f32[2,64,128]{1,0,2:T(2,128)S(1)} %get-tuple-element.84, f32[3,64,128]{1,0,2:T(4,128)} %get-tuple-element.82, ...), kind=kLoop, calls=%fused_computation.59 | loop fusion | flops 22413312 | bytes 24887488 | tf_op jit(solution)/shard_map/add | solution.py:62
  274.2 2.4 copy.174
  (63 shorter events, 14.2 us)
Async XLA Ops:
  0.6 11.9 %copy-start.13 = (f32[16,64,128]{2,1,0:T(8,128)S(1)}, f32[16,64,128]{2,1,0:T(8,128)}, u32[]{:S(2)}) copy-start(f32[16,64,128]{2,1,0:T(8,128)} %param.3) | copy-start | bytes 1572868
  1.7 30.3 %collective-permute-start = (f32[16,15,128]{2,0,1:T(8,128)S(1)}, f32[16,15,128]{2,0,1:T(8,128)S(1)}, u32[]{:S(2)}, u32[]{:S(2)}) collective-permute-start(f32[16,15,128]{2,0,1:T(8,128)S(1)} %copy.175), channel_id=1, source_target_pairs={{16,0},{32,16},{48,32},{64,48},{80,64},{96,80},{112,96},{128,112},... | collective-permute-start | bytes 368648 | tf_op jit(solution)/shard_map/ppermute | solution.py:18
  10.6 27.7 %collective-permute-start.1 = (f32[16,15,128]{2,0,1:T(8,128)S(1)}, f32[16,15,128]{2,0,1:T(8,128)}, u32[]{:S(2)}, u32[]{:S(2)}) collective-permute-start(f32[16,15,128]{2,0,1:T(8,128)S(1)} %copy.176), channel_id=1, source_target_pairs={{0,16},{16,32},{32,48},{48,64},{64,80},{80,96},{96,112},{112,128},... | collective-permute-start | bytes 368648 | tf_op jit(solution)/shard_map/ppermute | solution.py:15
  16.2 37.2 %copy-start.15 = (f32[4,64,128]{1,0,2:T(4,128)}, f32[4,64,128]{1,0,2:T(4,128)S(1)}, u32[]{:S(2)}) copy-start(f32[4,64,128]{1,0,2:T(4,128)S(1)} %get-tuple-element.80) | copy-start | bytes 393220
  23.1 6.4 %copy-start.3 = (f32[10,64,128]{1,0,2:T(8,128)}, f32[10,64,128]{1,0,2:T(8,128)S(1)}, u32[]{:S(2)}) copy-start(f32[10,64,128]{1,0,2:T(8,128)S(1)} %get-tuple-element.67) | copy-start | bytes 983044
  24.4 5.1 %copy-start.4 = (f32[11,64,128]{1,0,2:T(8,128)}, f32[11,64,128]{1,0,2:T(8,128)S(1)}, u32[]{:S(2)}) copy-start(f32[11,64,128]{1,0,2:T(8,128)S(1)} %get-tuple-element.65) | copy-start | bytes 1081348
  25.6 3.9 %copy-start.5 = (f32[12,64,128]{1,0,2:T(8,128)}, f32[12,64,128]{1,0,2:T(8,128)S(1)}, u32[]{:S(2)}) copy-start(f32[12,64,128]{1,0,2:T(8,128)S(1)} %get-tuple-element.63) | copy-start | bytes 1179652
  26.9 2.6 copy-start.6
  28.2 1.4 copy-start.7
  29.5 1.8 copy-start.8
  32.5 20.9 %copy-start = (f32[16,15,128]{1,0,2:T(8,128)}, f32[16,15,128]{1,0,2:T(8,128)S(1)}, u32[]{:S(2)}) copy-start(f32[16,15,128]{1,0,2:T(8,128)S(1)} %copy.120) | copy-start | bytes 368644
  39.7 1.1 copy-start.1
  39.7 13.8 %copy-start.2 = (f32[9,64,128]{1,0,2:T(8,128)S(1)}, f32[9,64,128]{1,0,2:T(8,128)}, u32[]{:S(2)}) copy-start(f32[9,64,128]{1,0,2:T(8,128)} %get-tuple-element.69) | copy-start | bytes 884740
  39.7 13.8 %copy-start.9 = (f32[7,64,128]{1,0,2:T(8,128)S(1)}, f32[7,64,128]{1,0,2:T(8,128)}, u32[]{:S(2)}) copy-start(f32[7,64,128]{1,0,2:T(8,128)} %get-tuple-element.74) | copy-start | bytes 688132
  39.7 13.8 %copy-start.10 = (f32[8,64,128]{1,0,2:T(8,128)S(1)}, f32[8,64,128]{1,0,2:T(8,128)}, u32[]{:S(2)}) copy-start(f32[8,64,128]{1,0,2:T(8,128)} %get-tuple-element.72) | copy-start | bytes 786436
  39.7 13.8 %copy-start.11 = (f32[5,64,128]{1,0,2:T(8,128)S(1)}, f32[5,64,128]{1,0,2:T(8,128)}, u32[]{:S(2)}) copy-start(f32[5,64,128]{1,0,2:T(8,128)} %get-tuple-element.78) | copy-start | bytes 491524
  39.7 13.8 %copy-start.12 = (f32[6,64,128]{1,0,2:T(8,128)S(1)}, f32[6,64,128]{1,0,2:T(8,128)}, u32[]{:S(2)}) copy-start(f32[6,64,128]{1,0,2:T(8,128)} %get-tuple-element.76) | copy-start | bytes 589828
  40.8 26.8 %collective-permute-start.2 = (f32[16,94,15]{1,0,2:T(8,128)}, f32[16,94,15]{1,0,2:T(8,128)S(1)}, u32[]{:S(2)}, u32[]{:S(2)}) collective-permute-start(f32[16,94,15]{1,0,2:T(8,128)} %get-tuple-element.55), channel_id=1, source_target_pairs={{1,0},{2,1},{3,2},{4,3},{5,4},{6,5},{7,6},{8,7},{9,8},{10,9},{11,1... | collective-permute-start | bytes 270728 | tf_op jit(solution)/shard_map/ppermute | solution.py:18
  51.4 17.4 %collective-permute-start.3 = (f32[16,94,15]{1,0,2:T(8,128)}, f32[16,94,15]{1,0,2:T(8,128)}, u32[]{:S(2)}, u32[]{:S(2)}) collective-permute-start(f32[16,94,15]{1,0,2:T(8,128)} %get-tuple-element.56), channel_id=1, source_target_pairs={{0,1},{1,2},{2,3},{3,4},{4,5},{5,6},{6,7},{7,8},{8,9},{9,10},{10,1... | collective-permute-start | bytes 270728 | tf_op jit(solution)/shard_map/ppermute | solution.py:15
  67.6 4.6 %copy-start.14 = (f32[3,64,128]{1,0,2:T(4,128)S(1)}, f32[3,64,128]{1,0,2:T(4,128)}, u32[]{:S(2)}) copy-start(f32[3,64,128]{1,0,2:T(4,128)} %get-tuple-element.82) | copy-start | bytes 294916
  67.6 4.6 %copy-start.16 = (f32[1,64,128]{1,0,2:T(1,128)S(1)}, f32[1,64,128]{1,0,2:T(1,128)}, u32[]{:S(2)}) copy-start(f32[1,64,128]{1,0,2:T(1,128)} %get-tuple-element.86) | copy-start | bytes 98308
  67.6 0.6 copy-start.17
  72.1 133.8 %copy-start.18 = (f32[3,16]{1,0:T(4,128)S(1)}, f32[3,16]{1,0:T(4,128)}, u32[]{:S(2)}) copy-start(f32[3,16]{1,0:T(4,128)} %param.5) | copy-start | bytes 580
  72.1 133.8 %copy-start.19 = (f32[3,16]{1,0:T(4,128)S(1)}, f32[3,16]{1,0:T(4,128)}, u32[]{:S(2)}) copy-start(f32[3,16]{1,0:T(4,128)} %param.4) | copy-start | bytes 580
where the time goes:
time: 278 us; the launch traced here: 277 us
  blocking collectives  108 us (39%)
  other arithmetic  87.8 us (32%)
  local copies, waits for them, and re-layouts  55.6 us (20%)
  starting transfers between devices  23.4 us (8%)
    psum x1, blocking collectives, on_device(): totals = lax.psum(partial_sums, ('gy', 'gx'))  108 us
    add x1, other arithmetic, on_device(): gradient = gradient + coefficient[2, step] * (forward_cols + backward_cols)  65.6 us
    ppermute x2, starting transfers between devices, with_halo(): lax.ppermute(lax.slice_in_dim(block, 0, width, axis=dim), axis, backward)  19.4 us
    another operation x1, local copies, waits for them, and re-layouts, on_device(): jnp.stack(plane_terms)  10.2 us
    another operation x1, local copies, waits for them, and re-layouts, on_device(): jnp.stack(col_terms)  10 us
    another operation x1, local copies, waits for them, and re-layouts, on_device(): jnp.stack(row_terms)  9.89 us
    reduce_sum x2, other arithmetic, on_device(): jnp.sum(field * along_rows[:, width + step:width + step + rows, :])  9.84 us
    slice x7, local copies, waits for them, and re-layouts, plane_shift(): return jnp.concatenate([field[by:], zeros], axis=0)  9.02 us
  transfers between devices with their start and end apart: 4, of which 1 were waited for; matrix products, arithmetic and copies ran while one was open for 14% of the time, Pallas kernels for 0%

commit v1 on v0

v1 whole, which is shorter than its diff:
```python
import numpy as np
import jax
import jax.numpy as jnp
from jax import lax
from jax.sharding import Mesh, PartitionSpec as P

OFFSETS = 16
GY = ("zl", "y", "c")
GX = ("x", "zh")


def shift(block, axes, forward):
    count = lax.axis_size(axes)
    step = 1 if forward else count - 1
    return lax.ppermute(block, axes, [(i, (i + step) % count) for i in range(count)])


def plane_shift(field, by):
    planes = field.shape[0]
    zeros = jnp.zeros((abs(by),) + field.shape[1:], jnp.float32)
    if by > 0:
        return jnp.concatenate([field[by:], zeros], axis=0)
    if by < 0:
        return jnp.concatenate([zeros, field[: planes + by]], axis=0)
    return field


def group_sum(values, axes):
    count = lax.axis_size(axes)
    copies = jnp.broadcast_to(values[None], (count,) + values.shape)
    return lax.all_to_all(copies, axes, 0, 0).sum(0)


def on_device(field, targets, weights):
    planes, rows, cols = field.shape
    width = OFFSETS - 1
    voxels = planes * rows * cols * lax.axis_size(GY + GX)
    right = shift(field[:, :, :width], GX, False)
    below = shift(field[:, :width, :], GY, False)
    left = shift(field[:, :, cols - width :], GX, True)
    above = shift(field[:, rows - width :, :], GY, True)
    along_rows = jnp.concatenate([above, field, below], axis=1)
    along_cols = jnp.concatenate([left, field, right], axis=2)
    plane_terms = []
    row_terms = []
    col_terms = []
    for step in range(OFFSETS):
        plane_terms.append(jnp.sum(field * plane_shift(field, step)))
        row_terms.append(jnp.sum(field * along_rows[:, width + step : width + step + rows, :]))
        col_terms.append(jnp.sum(field * along_cols[:, :, width + step : width + step + cols]))
    partial_sums = jnp.stack([jnp.stack(plane_terms), jnp.stack(row_terms), jnp.stack(col_terms)])
    packed = jnp.pad(partial_sums, ((0, 5), (0, 112)))
    totals = group_sum(group_sum(packed, ("c", "y", "x")), ("zl", "zh"))[:3, :OFFSETS]
    correlation = totals / jnp.float32(voxels)
    coefficient = weights * (correlation - targets)
    gradient = jnp.zeros_like(field)
    for step in range(OFFSETS):
        gradient = gradient + coefficient[0, step] * (
            plane_shift(field, step) + plane_shift(field, -step)
        )
    for step in range(OFFSETS):
        forward_rows = along_rows[:, width + step : width + step + rows, :]
        backward_rows = along_rows[:, width - step : width - step + rows, :]
        forward_cols = along_cols[:, :, width + step : width + step + cols]
        backward_cols = along_cols[:, :, width - step : width - step + cols]
        gradient = gradient + coefficient[1, step] * (forward_rows + backward_rows)
        gradient = gradient + coefficient[2, step] * (forward_cols + backward_cols)
    return (gradient, correlation)


def solution(mesh):
    devices = np.asarray(mesh.devices).reshape(4, 4, 2, 4, 4)
    fine = Mesh(devices, GY + GX)
    return jax.shard_map(
        on_device,
        mesh=fine,
        in_specs=(P(None, GY, GX), P(), P()),
        out_specs=(P(None, GY, GX), P()),
        check_vma=False,
    )
```

time: 278 us -> 226 us (0.81)
  the two profiles are of different devices: /device:TPU:1 before, /device:TPU:32 now
where the time goes in v1:
time: 226 us; the launch traced here: 225 us
  waiting for transfers between devices  70 us (31%)
  other arithmetic  53.5 us (24%)
  local copies, waits for them, and re-layouts  47.6 us (21%)
  starting transfers between devices  41 us (18%)
  blocking collectives  11.7 us (5%)
    ppermute x4, waiting for transfers between devices, shift(): lax.ppermute(block, axes, [(i, (i + step) % count) for i in range(count)])  66.9 us
    add x1, other arithmetic, on_device(): gradient = gradient + coefficient[2, step] * (forward_cols + backward_cols)  45 us
    ppermute x4, starting transfers between devices, shift(): lax.ppermute(block, axes, [(i, (i + step) % count) for i in range(count)])  28 us
    all_to_all x1, starting transfers between devices, group_sum(): return lax.all_to_all(copies, axes, 0, 0).sum(0)  13 us
    all_to_all x1, blocking collectives, group_sum(): return lax.all_to_all(copies, axes, 0, 0).sum(0)  11.7 us
    slice x14, local copies, waits for them, and re-layouts, plane_shift(): return jnp.concatenate([zeros, field[:planes + by]], axis=0)  10.8 us
    another operation x1, local copies, waits for them, and re-layouts, on_device(): jnp.stack(row_terms)  10.1 us
    another operation x1, local copies, waits for them, and re-layouts, on_device(): jnp.stack(plane_terms)  10.1 us
  transfers between devices with their start and end apart: 5, of which 4 were waited for; matrix products, arithmetic and copies ran while one was open for 9% of the time, Pallas kernels for 0%

profile of v1, /device:TPU:32, one launch (start us, length us, event | category | flops | bytes accessed | tf_op | source)
XLA Modules:
  0.0 224.5 jit_solution(12636634460164316279)
XLA Ops:
  0.6 1.7 fusion.163
  2.3 3.9 %collective-permute-start = (f32[16,15,128]{2,1,0:T(8,128)S(1)}, f32[16,15,128]{2,1,0:T(8,128)S(1)}, u32[]{:S(2)}, u32[]{:S(2)}) collective-permute-start(f32[16,15,128]{2,1,0:T(8,128)S(1)} %get-tuple-element.52), channel_id=1, source_target_pairs={{0,496},{16,0},{32,16},{48,32},{64,48},{80,64},{96,80},{112,96},{1... | collective-permute-start | bytes 368648 | tf_op jit(solution)/shard_map/ppermute | solution.py:15
  6.3 1.0 fusion.164
  7.3 14.9 %collective-permute-start.1 = (f32[16,64,15]{2,1,0:T(8,128)S(1)}, f32[16,64,15]{2,1,0:T(8,128)S(1)}, u32[]{:S(2)}, u32[]{:S(2)}) collective-permute-start(f32[16,64,15]{2,1,0:T(8,128)S(1)} %get-tuple-element.54), channel_id=1, source_target_pairs={{0,15},{1,0},{2,1},{3,2},{4,3},{5,4},{6,5},{7,6},{8,7},{9,8},{10,9... | collective-permute-start | bytes 184328 | tf_op jit(solution)/shard_map/ppermute | solution.py:15
  22.2 0.9 fusion.165
  23.1 0.9 fusion.166
  24.8 0.9 fusion.168
  25.7 0.9 fusion.169
  33.3 1.3 fusion.37
  35.3 2.0 multiply_reduce_fusion.15
  37.2 27.5 %collective-permute-done.1 = f32[16,64,15]{2,1,0:T(8,128)S(1)} collective-permute-done((f32[16,64,15]{2,1,0:T(8,128)S(1)}, f32[16,64,15]{2,1,0:T(8,128)S(1)}, u32[]{:S(2)}, u32[]{:S(2)}) %collective-permute-start.1) | collective-permute-done | bytes 61472 | tf_op jit(solution)/shard_map/ppermute | solution.py:15
  64.8 2.8 %multiply_reduce_fusion = (f32[]{:T(128)}, f32[]{:T(128)}, f32[]{:T(128)}, f32[]{:T(128)}, f32[]{:T(128)}, /*index=5*/f32[]{:T(128)}, f32[]{:T(128)}, f32[]{:T(1...) fusion(f32[16,64,128]{2,1,0:T(8,128)S(1)} %copy-done, ...), kind=kLoop, calls=%fused_computation.250 | loop fusion | flops 4718574 | bytes 8585288 | tf_op jit(solution)/shard_map/reduce_sum | solution.py:50
  67.6 10.1 %stack.177 = f32[16]{0:T(128)S(1)} concatenate(f32[1]{0:T(128)} %bitcast, f32[1]{0:T(128)} %bitcast.1, f32[1]{0:T(128)} %bitcast.2, f32[1]{0:T(128)} %bitcast.3, f32[1]{0:T(128)} %bitcast.4, f32[1]{0:T(128)} %bitcast.5, f32[1]{0:T(128)} %bitcast.6, f32[1]{0:T(128)} %bitcast.7, f32[1]{0:T(128)} %bitcast.8, f32[1]{0:T(128)} %bitcast.9, f32[1]{0:T(128)} %bitcast.10, f32[1]{0:T(128)} %bitcast.11, ...), dimensions={0} | concatenate | bytes 128 | tf_op jit(solution)/shard_map/stack | solution.py:51
  77.7 10.1 %stack.194 = f32[16]{0:T(128)S(1)} concatenate(f32[1]{0:T(128)} %bitcast, f32[1]{0:T(128)} %bitcast.17, f32[1]{0:T(128)} %bitcast.18, f32[1]{0:T(128)} %bitcast.19, f32[1]{0:T(128)} %bitcast.20, f32[1]{0:T(128)} %bitcast.21, f32[1]{0:T(128)} %bitcast.22, f32[1]{0:T(128)} %bitcast.23, f32[1]{0:T(128)} %bitcast.24, f32[1]{0:T(128)} %bitcast.25, f32[1]{0:T(128)} %bitcast.26, ...), dimensions={0} | concatenate | bytes 128 | tf_op jit(solution)/shard_map/stack | solution.py:51
  87.9 10.1 %stack.211 = f32[16]{0:T(128)S(1)} concatenate(f32[1]{0:T(128)} %bitcast, f32[1]{0:T(128)} %bitcast.33, f32[1]{0:T(128)} %bitcast.34, f32[1]{0:T(128)} %bitcast.35, f32[1]{0:T(128)} %bitcast.36, f32[1]{0:T(128)} %bitcast.37, f32[1]{0:T(128)} %bitcast.38, f32[1]{0:T(128)} %bitcast.39, f32[1]{0:T(128)} %bitcast.40, f32[1]{0:T(128)} %bitcast.41, f32[1]{0:T(128)} %bitcast.42, ...), dimensions={0} | concatenate | bytes 128 | tf_op jit(solution)/shard_map/stack | solution.py:51
  98.0 11.7 %all_to_all.10 = f32[32,8,128]{2,1,0:T(8,128)} all-to-all(f32[32,8,128]{2,1,0:T(8,128)S(1)} %broadcast_in_dim.4), channel_id=1, replica_groups=mesh['zl'=4,'y'=4,'c'=2,'x'=4,'zh'=4] {'c','y','x'}, dimensions={0} | all-to-all | bytes 262144 | tf_op jit(solution)/shard_map/all_to_all | solution.py:31
  109.7 0.9 reduce_sum.486
  111.2 13.0 %all-to-all-start.1 = ((f32[16,8,128]{2,1,0:T(8,128)}), f32[16,8,128]{2,1,0:T(8,128)}, u32[]{:S(2)}, u32[]{:S(2)}) async-start(f32[16,8,128]{2,1,0:T(8,128)} %broadcast_in_dim.5), calls=%async_computation.1 | async-start | bytes 131072 | tf_op jit(solution)/shard_map/all_to_all | solution.py:31
  124.2 7.3 %collective-permute-start.3 = (f32[16,64,15]{2,1,0:T(8,128)}, f32[16,64,15]{2,1,0:T(8,128)}, u32[]{:S(2)}, u32[]{:S(2)}) collective-permute-start(f32[16,64,15]{2,1,0:T(8,128)} %get-tuple-element.55), channel_id=1, source_target_pairs={{0,1},{1,2},{2,3},{3,4},{4,5},{5,6},{6,7},{7,8},{8,9},{9,10},{10,1... | collective-permute-start | bytes 184328 | tf_op jit(solution)/shard_map/ppermute | solution.py:15
  131.5 1.9 collective-permute-start.2
  133.4 3.1 %all-to-all-done.1 = f32[16,8,128]{2,1,0:T(8,128)} async-done(((f32[16,8,128]{2,1,0:T(8,128)}), f32[16,8,128]{2,1,0:T(8,128)}, u32[]{:S(2)}, u32[]{:S(2)}) %all-to-all-start.1) | async-done | bytes 65568 | tf_op jit(solution)/shard_map/all_to_all | solution.py:31
  140.1 35.7 %collective-permute-done.3 = f32[16,64,15]{2,1,0:T(8,128)} collective-permute-done((f32[16,64,15]{2,1,0:T(8,128)}, f32[16,64,15]{2,1,0:T(8,128)}, u32[]{:S(2)}, u32[]{:S(2)}) %collective-permute-start.3) | collective-permute-done | bytes 61472 | tf_op jit(solution)/shard_map/ppermute | solution.py:15
  175.8 3.7 %collective-permute-done.2 = f32[16,15,128]{2,1,0:T(8,128)} collective-permute-done((f32[16,15,128]{2,1,0:T(8,128)}, f32[16,15,128]{2,1,0:T(8,128)}, u32[]{:S(2)}, u32[]{:S(2)}) %collective-permute-start.2) | collective-permute-done | bytes 122912 | tf_op jit(solution)/shard_map/ppermute | solution.py:15
  179.5 45.0 %fusion.57 = f32[16,64,128]{2,1,0:T(8,128)} fusion(f32[16,64,128]{2,1,0:T(8,128)S(1)} %copy-done, f32[16,15,128]{2,1,0:T(8,128)} %collective-permute-done.2, f32[16,64,15]{2,1,0:T(8,128)} %collective-permute-done.3, f32[1,64,128]{2,1,0:T(8,128)} %copy-done.13, f32[2,64,128]{2,1,0:T(8,128)} %copy-done.12, f32[3,64,128]{2,1,0:T(8,128)} %copy-done.11, ...), kind=kLoop, calls=%fused_computation.141 | loop fusion | flops 22413312 | bytes 24826048 | tf_op jit(solution)/shard_map/add | solution.py:67
  (54 shorter events, 12.5 us)
Async XLA Ops:
  0.6 5.6 %copy-start = (f32[16,64,128]{2,1,0:T(8,128)S(1)}, f32[16,64,128]{2,1,0:T(8,128)}, u32[]{:S(2)}) copy-start(f32[16,64,128]{2,1,0:T(8,128)} %param.3) | copy-start | bytes 1572868
  2.3 32.9 %collective-permute-start = (f32[16,15,128]{2,1,0:T(8,128)S(1)}, f32[16,15,128]{2,1,0:T(8,128)S(1)}, u32[]{:S(2)}, u32[]{:S(2)}) collective-permute-start(f32[16,15,128]{2,1,0:T(8,128)S(1)} %get-tuple-element.52), channel_id=1, source_target_pairs={{0,496},{16,0},{32,16},{48,32},{64,48},{80,64},{96,80},{112,96},{1... | collective-permute-start | bytes 368648 | tf_op jit(solution)/shard_map/ppermute | solution.py:15
  7.3 57.5 %collective-permute-start.1 = (f32[16,64,15]{2,1,0:T(8,128)S(1)}, f32[16,64,15]{2,1,0:T(8,128)S(1)}, u32[]{:S(2)}, u32[]{:S(2)}) collective-permute-start(f32[16,64,15]{2,1,0:T(8,128)S(1)} %get-tuple-element.54), channel_id=1, source_target_pairs={{0,15},{1,0},{2,1},{3,2},{4,3},{5,4},{6,5},{7,6},{8,7},{9,8},{10,9... | collective-permute-start | bytes 184328 | tf_op jit(solution)/shard_map/ppermute | solution.py:15
  24.8 8.5 %copy-start.1 = (f32[13,64,128]{2,1,0:T(8,128)}, f32[13,64,128]{2,1,0:T(8,128)S(1)}, u32[]{:S(2)}) copy-start(f32[13,64,128]{2,1,0:T(8,128)S(1)} %get-tuple-element.61) | copy-start | bytes 1277956
  25.7 7.6 %copy-start.2 = (f32[12,64,128]{2,1,0:T(8,128)}, f32[12,64,128]{2,1,0:T(8,128)S(1)}, u32[]{:S(2)}) copy-start(f32[12,64,128]{2,1,0:T(8,128)S(1)} %get-tuple-element.63) | copy-start | bytes 1179652
  27.3 6.0 %copy-start.3 = (f32[10,64,128]{2,1,0:T(8,128)}, f32[10,64,128]{2,1,0:T(8,128)S(1)}, u32[]{:S(2)}) copy-start(f32[10,64,128]{2,1,0:T(8,128)S(1)} %get-tuple-element.67) | copy-start | bytes 983044
  28.1 5.2 %copy-start.4 = (f32[9,64,128]{2,1,0:T(8,128)}, f32[9,64,128]{2,1,0:T(8,128)S(1)}, u32[]{:S(2)}) copy-start(f32[9,64,128]{2,1,0:T(8,128)S(1)} %get-tuple-element.69) | copy-start | bytes 884740
  28.9 4.4 %copy-start.5 = (f32[8,64,128]{2,1,0:T(8,128)}, f32[8,64,128]{2,1,0:T(8,128)S(1)}, u32[]{:S(2)}) copy-start(f32[8,64,128]{2,1,0:T(8,128)S(1)} %get-tuple-element.71) | copy-start | bytes 786436
  29.7 3.6 %copy-start.7 = (f32[7,64,128]{2,1,0:T(8,128)}, f32[7,64,128]{2,1,0:T(8,128)S(1)}, u32[]{:S(2)}) copy-start(f32[7,64,128]{2,1,0:T(8,128)S(1)} %get-tuple-element.73) | copy-start | bytes 688132
  30.5 4.7 %copy-start.8 = (f32[6,64,128]{2,1,0:T(8,128)}, f32[6,64,128]{2,1,0:T(8,128)S(1)}, u32[]{:S(2)}) copy-start(f32[6,64,128]{2,1,0:T(8,128)S(1)} %get-tuple-element.75) | copy-start | bytes 589828
  31.2 4.0 %copy-start.9 = (f32[5,64,128]{2,1,0:T(8,128)}, f32[5,64,128]{2,1,0:T(8,128)S(1)}, u32[]{:S(2)}) copy-start(f32[5,64,128]{2,1,0:T(8,128)S(1)} %get-tuple-element.77) | copy-start | bytes 491524
  32.0 3.3 %copy-start.10 = (f32[4,64,128]{2,1,0:T(8,128)}, f32[4,64,128]{2,1,0:T(8,128)S(1)}, u32[]{:S(2)}) copy-start(f32[4,64,128]{2,1,0:T(8,128)S(1)} %get-tuple-element.79) | copy-start | bytes 393220
  32.6 32.1 %copy-start.11 = (f32[3,64,128]{2,1,0:T(8,128)}, f32[3,64,128]{2,1,0:T(8,128)S(1)}, u32[]{:S(2)}) copy-start(f32[3,64,128]{2,1,0:T(8,128)S(1)} %get-tuple-element.81) | copy-start | bytes 294916
  33.3 31.5 %copy-start.12 = (f32[2,64,128]{2,1,0:T(8,128)}, f32[2,64,128]{2,1,0:T(8,128)S(1)}, u32[]{:S(2)}) copy-start(f32[2,64,128]{2,1,0:T(8,128)S(1)} %get-tuple-element.83) | copy-start | bytes 196612
  35.2 29.6 %copy-start.13 = (f32[1,64,128]{2,1,0:T(8,128)}, f32[1,64,128]{2,1,0:T(8,128)S(1)}, u32[]{:S(2)}) copy-start(f32[1,64,128]{2,1,0:T(8,128)S(1)} %get-tuple-element.85) | copy-start | bytes 98308
  111.2 25.3 %all-to-all-start.1 = ((f32[16,8,128]{2,1,0:T(8,128)}), f32[16,8,128]{2,1,0:T(8,128)}, u32[]{:S(2)}, u32[]{:S(2)}) async-start(f32[16,8,128]{2,1,0:T(8,128)} %broadcast_in_dim.5), calls=%async_computation.1 | async-start | bytes 131072 | tf_op jit(solution)/shard_map/all_to_all | solution.py:31
  124.2 51.6 %collective-permute-start.3 = (f32[16,64,15]{2,1,0:T(8,128)}, f32[16,64,15]{2,1,0:T(8,128)}, u32[]{:S(2)}, u32[]{:S(2)}) collective-permute-start(f32[16,64,15]{2,1,0:T(8,128)} %get-tuple-element.55), channel_id=1, source_target_pairs={{0,1},{1,2},{2,3},{3,4},{4,5},{5,6},{6,7},{7,8},{8,9},{9,10},{10,1... | collective-permute-start | bytes 184328 | tf_op jit(solution)/shard_map/ppermute | solution.py:15
  131.5 5.9 %copy-start.14 = (f32[3,16]{1,0:T(4,128)S(1)}, f32[3,16]{1,0:T(4,128)}, u32[]{:S(2)}) copy-start(f32[3,16]{1,0:T(4,128)} %param.5) | copy-start | bytes 580
  131.5 5.9 %copy-start.15 = (f32[3,16]{1,0:T(4,128)S(1)}, f32[3,16]{1,0:T(4,128)}, u32[]{:S(2)}) copy-start(f32[3,16]{1,0:T(4,128)} %param.4) | copy-start | bytes 580
  131.5 48.0 %collective-permute-start.2 = (f32[16,15,128]{2,1,0:T(8,128)}, f32[16,15,128]{2,1,0:T(8,128)}, u32[]{:S(2)}, u32[]{:S(2)}) collective-permute-start(f32[16,15,128]{2,1,0:T(8,128)} %get-tuple-element.53), channel_id=1, source_target_pairs={{0,16},{16,32},{32,48},{48,64},{64,80},{80,96},{96,112},{112,128},... | collective-permute-start | bytes 368648 | tf_op jit(solution)/shard_map/ppermute | solution.py:15
  137.4 42.1 %copy-start.6 = (f32[8,64,128]{2,1,0:T(8,128)S(1)}, f32[8,64,128]{2,1,0:T(8,128)}, u32[]{:S(2)}) copy-start(f32[8,64,128]{2,1,0:T(8,128)} %copy-done.5) | copy-start | bytes 786436

commit v2 on v1

v2 whole, which is shorter than its diff:
```python
import jax
import jax.numpy as jnp
import numpy as np
from jax import lax
from jax.experimental import pallas as pl
from jax.experimental.pallas import tpu as pltpu
from jax.sharding import Mesh, PartitionSpec as P

OFFSETS = 16
GY = ("zl", "y", "c")
GX = ("x", "zh")
PLANE = ("c", "y", "x")
LINE = ("zl", "zh")
PLANES, ROWS, COLS = 16, 64, 128
GROUPS = 8
F32, BF16 = jnp.float32, jnp.bfloat16
HBM_SPEC = pl.BlockSpec(memory_space=pl.ANY)


def iota(shape, dim):
    return lax.broadcasted_iota(jnp.int32, shape, dim)


def halves(values):
    high = values.astype(BF16)
    return high, (values - high.astype(F32)).astype(BF16)


def contract(left, right, dims):
    return lax.dot_general(left, right, (dims, ((), ())), preferred_element_type=F32)


def quadrants(gram):
    half = gram.shape[0] // 2
    tall = gram[:half] + gram[half:]
    return tall[:, :half] + tall[:, half:] if half == 128 else tall + pltpu.roll(tall, half, 1)


def diagonal_sums(gram, keep, base):
    gram = jnp.where(keep, gram, 0.0)
    total = jnp.zeros((8, 128), F32)
    for block in range(gram.shape[0] // 8):
        by = (base - 8 * block) % 128
        values = gram[8 * block : 8 * block + 8]
        total = total + (pltpu.roll(values, by, 1) if by else values)
    row = iota((8, 128), 0)
    for bit in (1, 2, 4):
        total = jnp.where(row & bit != 0, pltpu.roll(total, 128 - bit, 1), total)
    return jnp.sum(total, axis=0, keepdims=True)


def edges_kernel(field, top, bottom, first, last):
    top[...] = field[:, :OFFSETS, :]
    bottom[...] = field[:, ROWS - OFFSETS :, :]
    block = iota((128, COLS), 1) // OFFSETS
    first_cols = jnp.zeros((128, COLS), F32)
    last_cols = jnp.zeros((128, COLS), F32)
    for group in range(GROUPS):
        values = field[2 * group : 2 * group + 2].reshape(128, COLS)
        moved = pltpu.roll(values, OFFSETS * group, 1) if group else values
        first_cols = jnp.where(block == group, moved, first_cols)
        last_cols = jnp.where(block == (group + 7) % 8, moved, last_cols)
    first[...] = first_cols
    last[...] = last_cols


def inner_kernel(field, out):
    gram = jnp.zeros((256, 256), F32)
    for part in range(ROWS // 8):
        values = field[:, 8 * part : 8 * part + 8, :].reshape(128, COLS)
        both = jnp.concatenate(halves(values), axis=0)
        gram = gram + contract(both, both, ((1,), (1,)))
    row, col = iota((128, 128), 0), iota((128, 128), 1)
    spread = diagonal_sums(quadrants(gram), (row % 8 == col % 8) & (col >= row), 0)
    gram = jnp.zeros((128, 128), F32)
    for plane in range(PLANES):
        both = jnp.concatenate(halves(field[plane]), axis=0)
        gram = gram + contract(both, both, ((1,), (1,)))
    apart = (col - row)[:ROWS]
    along_rows = diagonal_sums(quadrants(gram), (apart >= 0) & (apart < OFFSETS) & (col[:ROWS] < ROWS), 0)
    gram = jnp.zeros((256, 256), F32)
    for group in range(GROUPS):
        both = jnp.concatenate(halves(field[2 * group : 2 * group + 2].reshape(128, COLS)), axis=1)
        gram = gram + contract(both, both, ((0,), (0,)))
    apart = col - row
    along_cols = diagonal_sums(quadrants(gram), (apart >= 0) & (apart < OFFSETS), 0)
    lane, offset = iota((OFFSETS, 128), 1), iota((OFFSETS, 128), 0)
    column = jnp.sum(jnp.where(lane == 8 * offset, spread, 0.0), axis=1, keepdims=True)
    along_planes = jnp.sum(jnp.where(lane == offset, column, 0.0), axis=0, keepdims=True)
    axis = iota((8, 128), 0)
    sums = jnp.where(axis == 0, along_planes, jnp.where(axis == 1, along_rows, along_cols))
    out[...] = jnp.where((axis < 3) & (iota((8, 128), 1) < OFFSETS), sums, 0.0)


def border_kernel(inner, bottom, below, last, right, out):
    row, col = iota((128, 128), 0), iota((128, 128), 1)
    gram = jnp.zeros((128, 128), F32)
    for planes in (slice(0, 8), slice(8, 16)):
        mine_high, mine_low = halves(bottom[planes].reshape(128, COLS))
        next_high, next_low = halves(below[planes].reshape(128, COLS))
        product = contract(mine_high, jnp.concatenate([next_high, next_low], axis=0), ((1,), (1,)))
        gram = gram + product[:, :128] + product[:, 128:]
        gram = gram + contract(mine_low, next_high, ((1,), (1,)))
    along_rows = diagonal_sums(gram, (row // 16 == col // 16) & (col < row), OFFSETS)
    mine = jnp.concatenate(halves(last[...]), axis=1)
    other = jnp.concatenate(halves(right[...]), axis=1)
    gram = quadrants(contract(mine, other, ((0,), (0,))))
    apart = (col - row + 128) % 128
    keep = ((row // 16 + 1) % 8 == col // 16) & (apart < OFFSETS) & (apart > 0)
    along_cols = diagonal_sums(gram, keep, 0)
    axis = iota((8, 128), 0)
    sums = jnp.where(axis == 1, along_rows, jnp.where(axis == 2, along_cols, 0.0))
    sums = jnp.where(iota((8, 128), 1) < OFFSETS, sums, 0.0) + inner[...]
    out[...] = jnp.broadcast_to(sums[None], out.shape)


def gradient_kernel(
    voxels, field, above, below, left, right, totals, targets, weights, gradient, correlation, result, sems
):
    value = jnp.sum(totals[...], axis=0) / jnp.float32(voxels)
    correlation[...] = value[:3, :OFFSETS]
    coefficient = weights[...] * (value - targets[...])
    lane, offset = iota((OFFSETS, 128), 1), iota((OFFSETS, 128), 0)

    def column(axis):
        return jnp.sum(
            jnp.where(lane == offset, coefficient[axis : axis + 1], 0.0), axis=1, keepdims=True
        )

    def line(values, lanes):
        return jnp.sum(jnp.where(lane == lanes, values, 0.0), axis=0, keepdims=True)

    def toeplitz(values, size, base):
        return pltpu.roll(
            jnp.broadcast_to(values, (size, 128)), base, 1, stride=1, stride_axis=0
        )

    back = (128 - offset) % 128
    by_plane, by_row, by_col = column(0), column(1), column(2)
    row, col = iota((128, 128), 0), iota((128, 128), 1)
    ahead = toeplitz(line(by_plane, 8 * offset), 128, 0)
    behind = toeplitz(line(by_plane, (128 - 8 * offset) % 128), 128, 0)
    plane_high, plane_low = halves(
        jnp.where(col == row, 2.0 * ahead, jnp.where(col > row, ahead, behind))
    )
    row_high, row_low = halves(
        toeplitz(line(by_row, offset) + line(by_row, back), ROWS, OFFSETS)
    )
    around = toeplitz(line(by_col, offset) + line(by_col, back), 128, 0)
    inside = jnp.abs(col - row) < OFFSETS
    col_high, col_low = halves(
        jnp.concatenate([jnp.where(inside, around, 0.0), jnp.where(inside, 0.0, around)], axis=0)
    )

    nn = ((1,), (0,))
    zeros = jnp.zeros((128, 128), BF16)
    plane_left = jnp.concatenate(
        [
            jnp.concatenate([plane_high, plane_high], axis=1),
            jnp.concatenate([plane_low, zeros], axis=1),
        ],
        axis=0,
    )
    for part in range(ROWS // 8):
        values = field[:, 8 * part : 8 * part + 8, :].reshape(128, COLS)
        both = jnp.concatenate(halves(values), axis=0)
        product = contract(plane_left, both, nn)
        result[:, 8 * part : 8 * part + 8, :] = (product[:128] + product[128:]).reshape(
            PLANES, 8, COLS
        )

    row_left = jnp.concatenate([row_high, row_low], axis=0)
    block = iota((128, COLS), 1) // OFFSETS
    copies = []
    for group in range(GROUPS):
        values = field[2 * group : 2 * group + 2].reshape(128, COLS)
        halo = jnp.where(block == group, right[...], left[...])
        if group:
            halo = pltpu.roll(halo, 128 - OFFSETS * group, 1)
        high, low = halves(jnp.concatenate([values, halo], axis=1))
        total = contract(high, col_high, nn) + contract(high, col_low, nn)
        total = total + contract(low, col_high, nn)
        parts = []
        for plane in (2 * group, 2 * group + 1):
            tall = jnp.concatenate(
                [above[plane], field[plane], below[plane], jnp.zeros((32, COLS), F32)], axis=0
            )
            high, low = halves(tall)
            product = contract(row_left, high, nn)
            parts.append(product[:ROWS] + product[ROWS:] + contract(row_high, low, nn))
        total = total + jnp.concatenate(parts, axis=0)
        planes = slice(2 * group, 2 * group + 2)
        result[planes] = result[planes] + total.reshape(2, ROWS, COLS)
        copy = pltpu.make_async_copy(result.at[planes], gradient.at[planes], sems.at[group])
        copy.start()
        copies.append(copy)
    for copy in copies:
        copy.wait()


def shift(block, axes, forward):
    count = lax.axis_size(axes)
    step = 1 if forward else count - 1
    return lax.ppermute(block, axes, [(i, (i + step) % count) for i in range(count)])


def shaped(*shape):
    return jax.ShapeDtypeStruct(shape, F32)


def on_device(field, targets, weights):
    voxels = PLANES * ROWS * COLS * lax.axis_size(GY + GX)
    plane_count, line_count = lax.axis_size(PLANE), lax.axis_size(LINE)
    targets = jnp.pad(targets, ((0, 5), (0, 128 - OFFSETS)))
    weights = jnp.pad(weights, ((0, 5), (0, 128 - OFFSETS)))
    edge = shaped(PLANES, OFFSETS, COLS)
    side = shaped(128, COLS)
    top, bottom, first, last = pl.pallas_call(
        edges_kernel, out_shape=(edge, edge, side, side), name="edges"
    )(field)
    right = shift(first, GX, False)
    below = shift(top, GY, False)
    left = shift(last, GX, True)
    above = shift(bottom, GY, True)
    inner = pl.pallas_call(
        inner_kernel,
        out_shape=shaped(8, 128),
        name="inner",
        cost_estimate=pl.CostEstimate(flops=600_000_000, bytes_accessed=1 << 19, transcendentals=0),
    )(field)
    sums = pl.pallas_call(border_kernel, out_shape=shaped(plane_count, 8, 128), name="border")(
        inner, bottom, below, last, right
    )
    sums = lax.all_to_all(sums, PLANE, 0, 0).sum(0)
    totals = lax.all_to_all(
        jnp.broadcast_to(sums[None], (line_count, 8, 128)), LINE, 0, 0
    )
    vmem = pl.BlockSpec(memory_space=pltpu.VMEM)
    return pl.pallas_call(
        lambda *refs: gradient_kernel(voxels, *refs),
        out_shape=(shaped(PLANES, ROWS, COLS), shaped(3, OFFSETS)),
        in_specs=[vmem] * 8,
        out_specs=(HBM_SPEC, vmem),
        scratch_shapes=[
            pltpu.VMEM((PLANES, ROWS, COLS), F32),
            pltpu.SemaphoreType.DMA((GROUPS,)),
        ],
        name="gradient",
    )(field, above, below, left, right, totals, targets, weights)


def solution(mesh):
    devices = np.asarray(mesh.devices).reshape(4, 4, 2, 4, 4)
    fine = Mesh(devices, GY + GX)
    return jax.shard_map(
        on_device,
        mesh=fine,
        in_specs=(P(None, GY, GX), P(), P()),
        out_specs=(P(None, GY, GX), P()),
        check_vma=False,
    )
```

time: 226 us -> 77.5 us (0.34)
  the two profiles are of different devices: /device:TPU:32 before, /device:TPU:1 now
where the time goes in v2:
time: 77.5 us; the launch traced here: 77 us
  starting transfers between devices  38.8 us (50%)
  blocking collectives  16.1 us (21%)
  Pallas kernels  10.8 us (14%)
  waiting for transfers between devices  6.61 us (9%)
  local copies, waits for them, and re-layouts  3.78 us (5%)
    ppermute x4, starting transfers between devices, shift(): lax.ppermute(block, axes, [(i, (i + step) % count) for i in range(count)])  28.4 us
    all_to_all x1, blocking collectives, on_device(): sums = lax.all_to_all(sums, PLANE, 0, 0).sum(0)  16.1 us
    all_to_all x1, starting transfers between devices, on_device(): lax.all_to_all(jnp.broadcast_to(sums[None], (line_count, 8, 128)), LINE,...  10.5 us
    ppermute x4, waiting for transfers between devices, shift(): lax.ppermute(block, axes, [(i, (i + step) % count) for i in range(count)])  6.61 us
    pallas_call x1, Pallas kernels, on_device(): pl.pallas_call(lambda *refs: gradient_kernel(voxels, *refs), out_shape=(s...  3.76 us
    pallas_call x1, Pallas kernels, on_device(): pl.pallas_call(inner_kernel, out_shape=shaped(8, 128), name='inner', cost...  2.95 us
    pallas_call x1, Pallas kernels, on_device(): pl.pallas_call(border_kernel, out_shape=shaped(plane_count, 8, 128), name...  2.23 us
    unnamed x18, local copies, waits for them, and re-layouts  1.96 us
  transfers between devices with their start and end apart: 5, of which 2 were waited for; matrix products, arithmetic and copies ran while one was open for 2% of the time, Pallas kernels for 4%

profile of v2, /device:TPU:1, one launch (start us, length us, event | category | flops | bytes accessed | tf_op | source)
XLA Modules:
  0.0 77.0 jit_solution(1760810782865695548)
XLA Ops:
  0.6 1.9 %edges.1 = (f32[16,16,128]{2,1,0:T(8,128)}, f32[16,16,128]{2,1,0:T(8,128)}, f32[128,128]{1,0:T(8,128)}, f32[128,128]{1,0:T(8,128)}) custom-call(f32[16,64,128]{2,1,0:T(8,128)} %refs_0_.1), custom_call_target="tpu_custom_call" | custom-call | tf_op jit(solution)/shard_map/edges/pallas_call | solution.py:218
  2.5 8.8 %collective-permute-start.1 = (f32[16,16,128]{2,1,0:T(8,128)}, f32[16,16,128]{2,1,0:T(8,128)S(1)}, u32[]{:S(2)}, u32[]{:S(2)}) collective-permute-start(f32[16,16,128]{2,1,0:T(8,128)} %get-tuple-element.7), channel_id=1, source_target_pairs={{0,496},{16,0},{32,16},{48,32},{64,48},{80,64},{96,80},{112,96},{1... | collective-permute-start | bytes 393224 | tf_op jit(solution)/shard_map/ppermute | solution.py:204
  11.3 9.3 %collective-permute-start.3 = (f32[128,128]{1,0:T(8,128)}, f32[128,128]{1,0:T(8,128)S(1)}, u32[]{:S(2)}, u32[]{:S(2)}) collective-permute-start(f32[128,128]{1,0:T(8,128)} %get-tuple-element.9), channel_id=1, source_target_pairs={{0,15},{1,0},{2,1},{3,2},{4,3},{5,4},{6,5},{7,6},{8,7},{9,8},{10,9... | collective-permute-start | bytes 196616 | tf_op jit(solution)/shard_map/ppermute | solution.py:204
  20.6 3.0 %inner.1 = f32[8,128]{1,0:T(8,128)} custom-call(f32[16,64,128]{2,1,0:T(8,128)} %refs_0_.1), custom_call_target="tpu_custom_call" | custom-call | flops 600000000 | bytes 524288 | tf_op jit(solution)/shard_map/inner/pallas_call | solution.py:225
  23.5 0.2 collective-permute-done.3.right.refs_4_
  23.7 0.0 collective-permute-done.1.below.refs_2_
  23.7 0.6 copy-done.2
  24.3 0.1 copy-done
  24.4 2.2 %border.1 = f32[32,8,128]{2,1,0:T(8,128)} custom-call(f32[8,128]{1,0:T(8,128)} %inner.1, f32[16,16,128]{2,1,0:T(8,128)} %get-tuple-element.6.bottom, f32[16,16,128]{2,1,0:T(8,128)} %copy-done, f32[128,128]{1,0:T(8,128)} %get-tuple-element.8.last, f32[128,128]{1,0:T(8,128)} %copy-done.2), custom_call_target="tpu_custom_call" | custom-call | tf_op jit(solution)/shard_map/border/pallas_call | solution.py:231
  26.6 16.1 %all_to_all.10 = f32[32,8,128]{2,1,0:T(8,128)S(1)} all-to-all(f32[32,8,128]{2,1,0:T(8,128)} %border.1), channel_id=1, replica_groups=mesh['zl'=4,'y'=4,'c'=2,'x'=4,'zh'=4] {'c','y','x'}, dimensions={0} | all-to-all | bytes 262144 | tf_op jit(solution)/shard_map/all_to_all | solution.py:234
  42.8 0.6 broadcast_in_dim.2
  43.4 10.5 %all-to-all-start.1 = ((f32[16,8,128]{2,1,0:T(8,128)}), f32[16,8,128]{2,1,0:T(8,128)S(1)}, u32[]{:S(2)}, u32[]{:S(2)}) async-start(f32[16,8,128]{2,1,0:T(8,128)} %broadcast_in_dim.2), calls=%async_computation.1 | async-start | bytes 131072 | tf_op jit(solution)/shard_map/all_to_all | solution.py:235
  53.9 0.0 copy-start.8
  53.9 2.9 %collective-permute-start = (f32[16,16,128]{2,1,0:T(8,128)S(1)}, f32[16,16,128]{2,1,0:T(8,128)S(1)}, u32[]{:S(2)}, u32[]{:S(2)}) collective-permute-start(f32[16,16,128]{2,1,0:T(8,128)S(1)} %copy-done.4), channel_id=1, source_target_pairs={{0,16},{16,32},{32,48},{48,64},{64,80},{80,96},{96,112},{112,128},... | collective-permute-start | bytes 393224 | tf_op jit(solution)/shard_map/ppermute | solution.py:204
  56.8 7.5 %collective-permute-start.2 = (f32[128,128]{1,0:T(8,128)S(1)}, f32[128,128]{1,0:T(8,128)S(1)}, u32[]{:S(2)}, u32[]{:S(2)}) collective-permute-start(f32[128,128]{1,0:T(8,128)S(1)} %copy-done.5), channel_id=1, source_target_pairs={{0,1},{1,2},{2,3},{3,4},{4,5},{5,6},{6,7},{7,8},{8,9},{9,10},{10,1... | collective-permute-start | bytes 196616 | tf_op jit(solution)/shard_map/ppermute | solution.py:204
  64.3 0.6 pad.7.refs_6_
  64.9 0.6 pad.8.refs_7_
  65.5 6.4 %collective-permute-done.2.refs_3_ = f32[128,128]{1,0:T(8,128)S(1)} collective-permute-done((f32[128,128]{1,0:T(8,128)S(1)}, f32[128,128]{1,0:T(8,128)S(1)}, u32[]{:S(2)}, u32[]{:S(2)}) %collective-permute-start.2) | collective-permute-done | bytes 65568 | tf_op jit(solution)/shard_map/ppermute | solution.py:204
  71.9 0.0 collective-permute-done.refs_1_
  71.9 0.0 all-to-all-done.1.refs_5_
  71.9 0.6 copy-done.6
  72.5 0.1 copy-done.3
  72.6 0.6 copy-done.1
  73.2 3.8 %gradient.1 = (f32[16,64,128]{2,1,0:T(8,128)}, f32[3,16]{1,0:T(4,128)}) custom-call(f32[16,64,128]{2,1,0:T(8,128)} %refs_0_.1, f32[16,16,128]{2,1,0:T(8,128)} %copy-done.3, f32[16,16,128]{2,1,0:T(8,128)} %copy-done, f32[128,128]{1,0:T(8,128)} %copy-done.6, f32[128,128]{1,0:T(8,128)} %copy-done.2, f32[16,8,128]{2,1,0:T(8,128)} %copy-done.1, ...), custom_call_target="tpu_custom_call" | custom-call | tf_op jit(solution)/shard_map/gradient/pallas_call | solution.py:239
  (13 shorter events, 0.1 us)
Async XLA Ops:
  2.5 21.2 %collective-permute-start.1 = (f32[16,16,128]{2,1,0:T(8,128)}, f32[16,16,128]{2,1,0:T(8,128)S(1)}, u32[]{:S(2)}, u32[]{:S(2)}) collective-permute-start(f32[16,16,128]{2,1,0:T(8,128)} %get-tuple-element.7), channel_id=1, source_target_pairs={{0,496},{16,0},{32,16},{48,32},{64,48},{80,64},{96,80},{112,96},{1... | collective-permute-start | bytes 393224 | tf_op jit(solution)/shard_map/ppermute | solution.py:204
  11.3 12.4 %collective-permute-start.3 = (f32[128,128]{1,0:T(8,128)}, f32[128,128]{1,0:T(8,128)S(1)}, u32[]{:S(2)}, u32[]{:S(2)}) collective-permute-start(f32[128,128]{1,0:T(8,128)} %get-tuple-element.9), channel_id=1, source_target_pairs={{0,15},{1,0},{2,1},{3,2},{4,3},{5,4},{6,5},{7,6},{8,7},{9,8},{10,9... | collective-permute-start | bytes 196616 | tf_op jit(solution)/shard_map/ppermute | solution.py:204
  23.7 0.6 copy-start.2
  23.7 0.7 copy-start
  42.8 11.1 %copy-start.4 = (f32[16,16,128]{2,1,0:T(8,128)S(1)}, f32[16,16,128]{2,1,0:T(8,128)}, u32[]{:S(2)}) copy-start(f32[16,16,128]{2,1,0:T(8,128)} %get-tuple-element.6.bottom) | copy-start | bytes 393220
  43.4 13.4 %copy-start.5 = (f32[128,128]{1,0:T(8,128)S(1)}, f32[128,128]{1,0:T(8,128)}, u32[]{:S(2)}) copy-start(f32[128,128]{1,0:T(8,128)} %get-tuple-element.8.last) | copy-start | bytes 196612
  43.4 20.8 %copy-start.7 = (f32[3,16]{1,0:T(4,128)S(1)}, f32[3,16]{1,0:T(4,128)}, u32[]{:S(2)}) copy-start(f32[3,16]{1,0:T(4,128)} %param.4) | copy-start | bytes 580
  43.4 28.5 %all-to-all-start.1 = ((f32[16,8,128]{2,1,0:T(8,128)}), f32[16,8,128]{2,1,0:T(8,128)S(1)}, u32[]{:S(2)}, u32[]{:S(2)}) async-start(f32[16,8,128]{2,1,0:T(8,128)} %broadcast_in_dim.2), calls=%async_computation.1 | async-start | bytes 131072 | tf_op jit(solution)/shard_map/all_to_all | solution.py:235
  53.9 10.9 %copy-start.8 = (f32[3,16]{1,0:T(4,128)S(1)}, f32[3,16]{1,0:T(4,128)}, u32[]{:S(2)}) copy-start(f32[3,16]{1,0:T(4,128)} %param.5) | copy-start | bytes 580
  53.9 18.0 %collective-permute-start = (f32[16,16,128]{2,1,0:T(8,128)S(1)}, f32[16,16,128]{2,1,0:T(8,128)S(1)}, u32[]{:S(2)}, u32[]{:S(2)}) collective-permute-start(f32[16,16,128]{2,1,0:T(8,128)S(1)} %copy-done.4), channel_id=1, source_target_pairs={{0,16},{16,32},{32,48},{48,64},{64,80},{80,96},{96,112},{112,128},... | collective-permute-start | bytes 393224 | tf_op jit(solution)/shard_map/ppermute | solution.py:204
  56.8 15.1 %collective-permute-start.2 = (f32[128,128]{1,0:T(8,128)S(1)}, f32[128,128]{1,0:T(8,128)S(1)}, u32[]{:S(2)}, u32[]{:S(2)}) collective-permute-start(f32[128,128]{1,0:T(8,128)S(1)} %copy-done.5), channel_id=1, source_target_pairs={{0,1},{1,2},{2,3},{3,4},{4,5},{5,6},{6,7},{7,8},{8,9},{9,10},{10,1... | collective-permute-start | bytes 196616 | tf_op jit(solution)/shard_map/ppermute | solution.py:204
  71.9 0.6 copy-start.6
  71.9 0.7 copy-start.3
  72.6 0.6 copy-start.1

commit v3 on v2

v3 whole, which is shorter than its diff:
```python
import jax
import jax.numpy as jnp
import numpy as np
from jax import lax
from jax.experimental import pallas as pl
from jax.experimental.pallas import tpu as pltpu
from jax.sharding import Mesh, PartitionSpec as P

OFFSETS = 16
GY = ("zl", "y", "c")
GX = ("x", "zh")
PLANE = ("c", "y", "x")
LINE = ("zl", "zh")
PLANES, ROWS, COLS = 16, 64, 128
GROUPS = 8
F32, BF16 = jnp.float32, jnp.bfloat16
PAY = 8
INNER, BORDER = 600_000_000, 2_000_000_000
HBM_SPEC = pl.BlockSpec(memory_space=pl.ANY)


def iota(shape, dim):
    return lax.broadcasted_iota(jnp.int32, shape, dim)


def halves(values):
    high = values.astype(BF16)
    return high, (values - high.astype(F32)).astype(BF16)


def contract(left, right, dims):
    return lax.dot_general(left, right, (dims, ((), ())), preferred_element_type=F32)


def quadrants(gram):
    half = gram.shape[0] // 2
    tall = gram[:half] + gram[half:]
    return tall[:, :half] + tall[:, half:] if half == 128 else tall + pltpu.roll(tall, half, 1)


def diagonal_sums(gram, keep, base):
    gram = jnp.where(keep, gram, 0.0)
    total = jnp.zeros((8, 128), F32)
    for block in range(gram.shape[0] // 8):
        by = (base - 8 * block) % 128
        values = gram[8 * block : 8 * block + 8]
        total = total + (pltpu.roll(values, by, 1) if by else values)
    row = iota((8, 128), 0)
    for bit in (1, 2, 4):
        total = jnp.where(row & bit != 0, pltpu.roll(total, 128 - bit, 1), total)
    return jnp.sum(total, axis=0, keepdims=True)


def one_row(*sums):
    axis = iota((1, 128), 1) // OFFSETS
    row = jnp.where(axis == 0, sums[0], 0.0)
    for a in (1, 2):
        row = jnp.where(axis == a, pltpu.roll(sums[a], OFFSETS * a, 1), row)
    return row


def columns_kernel(field, first, last):
    block = iota((128, COLS), 1) // OFFSETS
    first_cols = jnp.zeros((128, COLS), F32)
    last_cols = jnp.zeros((128, COLS), F32)
    for group in range(GROUPS):
        values = field[2 * group : 2 * group + 2].reshape(128, COLS)
        moved = pltpu.roll(values, OFFSETS * group, 1) if group else values
        first_cols = jnp.where(block == group, moved, first_cols)
        last_cols = jnp.where(block == (group + 7) % 8, moved, last_cols)
    first[...] = first_cols
    last[...] = last_cols


def odd(axis):
    return lax.axis_index(axis) % 2 == 1


def swapped(flag, first, second):
    return jnp.where(flag, second, first), jnp.where(flag, first, second)


def rows_kernel(field, after, near_pair, far_pair):
    near_pair[...], far_pair[...] = swapped(
        odd("c"), field[:, ROWS - OFFSETS :, :], field[:, :OFFSETS, :]
    )


def again_kernel(first, after, out):
    out[...] = first[...]


def settle_kernel(right, after, out):
    out[...] = jnp.zeros_like(out)


def inner_kernel(field, out):
    gram = jnp.zeros((256, 256), F32)
    for part in range(ROWS // 8):
        values = field[:, 8 * part : 8 * part + 8, :].reshape(128, COLS)
        both = jnp.concatenate(halves(values), axis=0)
        gram = gram + contract(both, both, ((1,), (1,)))
    row, col = iota((128, 128), 0), iota((128, 128), 1)
    spread = diagonal_sums(quadrants(gram), (row % 8 == col % 8) & (col >= row), 0)
    gram = jnp.zeros((128, 128), F32)
    for plane in range(PLANES):
        both = jnp.concatenate(halves(field[plane]), axis=0)
        gram = gram + contract(both, both, ((1,), (1,)))
    apart = (col - row)[:ROWS]
    along_rows = diagonal_sums(quadrants(gram), (apart >= 0) & (apart < OFFSETS) & (col[:ROWS] < ROWS), 0)
    gram = jnp.zeros((256, 256), F32)
    for group in range(GROUPS):
        both = jnp.concatenate(halves(field[2 * group : 2 * group + 2].reshape(128, COLS)), axis=1)
        gram = gram + contract(both, both, ((0,), (0,)))
    apart = col - row
    along_cols = diagonal_sums(quadrants(gram), (apart >= 0) & (apart < OFFSETS), 0)
    lane, offset = iota((OFFSETS, 128), 1), iota((OFFSETS, 128), 0)
    column = jnp.sum(jnp.where(lane == 8 * offset, spread, 0.0), axis=1, keepdims=True)
    along_planes = jnp.sum(jnp.where(lane == offset, column, 0.0), axis=0, keepdims=True)
    out[...] = one_row(along_planes, along_rows, along_cols)


def border_cols_kernel(left, first, inner, out):
    row, col = iota((128, 128), 0), iota((128, 128), 1)
    mine = jnp.concatenate(halves(left[...]), axis=1)
    other = jnp.concatenate(halves(first[...]), axis=1)
    gram = quadrants(contract(mine, other, ((0,), (0,))))
    apart = (col - row + 128) % 128
    keep = ((row // 16 + 1) % 8 == col // 16) & (apart < OFFSETS) & (apart > 0)
    zeros = jnp.zeros((1, 128), F32)
    out[...] = inner[...] + one_row(zeros, zeros, diagonal_sums(gram, keep, 0))


def border_rows_kernel(mine_far, mine_near, row_far, row_near, sums, out):
    _, above = swapped(odd("c"), row_near[...], row_far[...])
    _, top = swapped(odd("c"), mine_near[...], mine_far[...])
    row, col = iota((128, 128), 0), iota((128, 128), 1)
    gram = jnp.zeros((128, 128), F32)
    for planes in (slice(0, 8), slice(8, 16)):
        mine_high, mine_low = halves(above[planes].reshape(128, COLS))
        next_high, next_low = halves(top[planes].reshape(128, COLS))
        product = contract(mine_high, jnp.concatenate([next_high, next_low], axis=0), ((1,), (1,)))
        gram = gram + product[:, :128] + product[:, 128:]
        gram = gram + contract(mine_low, next_high, ((1,), (1,)))
    zeros = jnp.zeros((1, 128), F32)
    along_rows = diagonal_sums(gram, (row // 16 == col // 16) & (col < row), OFFSETS)
    out[...] = jnp.broadcast_to((sums[...] + one_row(zeros, along_rows, zeros))[None], out.shape)


def gradient_kernel(
    voxels, field, row_far, row_near, left, right, totals, targets, weights, after, gradient, correlation, result, sems
):
    value = jnp.sum(totals[...], axis=0, keepdims=True) / jnp.float32(voxels)
    value = jnp.concatenate([value[:, OFFSETS * a : OFFSETS * (a + 1)] for a in range(3)], axis=0)
    correlation[...] = value
    coefficient = weights[...] * (value - targets[...])
    lane, offset = iota((OFFSETS, 128), 1), iota((OFFSETS, 128), 0)
    same = iota((OFFSETS, OFFSETS), 0) == iota((OFFSETS, OFFSETS), 1)

    def column(axis):
        return jnp.sum(
            jnp.where(same, coefficient[axis : axis + 1], 0.0), axis=1, keepdims=True
        )

    def line(values, lanes):
        return jnp.sum(jnp.where(lane == lanes, values, 0.0), axis=0, keepdims=True)

    def toeplitz(values, size, base):
        return pltpu.roll(
            jnp.broadcast_to(values, (size, 128)), base, 1, stride=1, stride_axis=0
        )

    def both(high, low):
        return jnp.concatenate(
            [
                jnp.concatenate([high, high], axis=1),
                jnp.concatenate([low, jnp.zeros_like(low)], axis=1),
            ],
            axis=0,
        )

    back = (128 - offset) % 128
    nn = ((1,), (0,))
    along_planes, along_rows, along_cols = column(0), column(1), column(2)
    row, col = iota((128, 128), 0), iota((128, 128), 1)
    around = toeplitz(line(along_cols, offset) + line(along_cols, back), 128, 0)
    inside = jnp.abs(col - row) < OFFSETS
    col_high, col_low = halves(
        jnp.concatenate([jnp.where(inside, around, 0.0), jnp.where(inside, 0.0, around)], axis=0)
    )
    row_left = both(
        *halves(
            toeplitz(line(along_rows, offset) + line(along_rows, back), ROWS, OFFSETS)[
                :, : ROWS + 32
            ]
        )
    )
    ahead = toeplitz(line(along_planes, 8 * offset), 128, 0)
    behind = toeplitz(line(along_planes, (128 - 8 * offset) % 128), 128, 0)
    plane_left = both(
        *halves(jnp.where(col == row, 2.0 * ahead, jnp.where(col > row, ahead, behind)))
    )
    below, above = swapped(odd("c"), row_near[...], row_far[...])

    for pair in range(ROWS // 16):
        parts = []
        for side in range(2):
            rows = slice(16 * pair + 8 * side, 16 * pair + 8 * side + 8)
            parts.append(jnp.concatenate(halves(field[:, rows, :].reshape(128, COLS)), axis=0))
        product = contract(plane_left, jnp.concatenate(parts, axis=1), nn)
        product = product[:128] + product[128:]
        for side in range(2):
            rows = slice(16 * pair + 8 * side, 16 * pair + 8 * side + 8)
            result[:, rows, :] = product[:, COLS * side : COLS * (side + 1)].reshape(PLANES, 8, COLS)

    block = iota((128, COLS), 1) // OFFSETS
    col_right = jnp.concatenate([col_high, col_low], axis=1)
    copies = []
    for group in range(GROUPS):
        values = field[2 * group : 2 * group + 2].reshape(128, COLS)
        halo = jnp.where(block == group, right[...], left[...])
        if group:
            halo = pltpu.roll(halo, 128 - OFFSETS * group, 1)
        high, low = halves(jnp.concatenate([values, halo], axis=1))
        product = contract(high, col_right, nn)
        total = product[:, :128] + product[:, 128:] + contract(low, col_high, nn)
        talls = []
        for plane in (2 * group, 2 * group + 1):
            tall = jnp.concatenate([above[plane], field[plane], below[plane]], axis=0)
            talls.append(jnp.concatenate(halves(tall), axis=0))
        product = contract(row_left, jnp.concatenate(talls, axis=1), nn)
        product = product[:ROWS] + product[ROWS:]
        total = total + jnp.concatenate([product[:, :COLS], product[:, COLS:]], axis=0)
        planes = slice(2 * group, 2 * group + 2)
        result[planes] = result[planes] + total.reshape(2, ROWS, COLS)
        copy = pltpu.make_async_copy(result.at[planes], gradient.at[planes], sems.at[group])
        copy.start()
        copies.append(copy)
    for copy in copies:
        copy.wait()


def middle_kernel(parts, out):
    total = jnp.sum(parts[...], axis=0)[:1]
    out[...] = jnp.broadcast_to(total, out.shape)


def shift(block, axes, forward):
    count = lax.axis_size(axes)
    step = 1 if forward else count - 1
    return lax.ppermute(block, axes, [(i, (i + step) % count) for i in range(count)])


def swap(block, axes, shift):
    count = lax.axis_size(axes)
    pairs = [(i, (i + 1) % count) for i in range(shift, count, 2)]
    return lax.ppermute(block, axes, [pair for i, j in pairs for pair in ((i, j), (j, i))])


def exchange(parts, axes):
    if parts.ndim == 2:
        return lax.all_to_all(parts[:, None], axes, 0, 0)[:, 0]
    return lax.all_to_all(parts, axes, 0, 0)


def resident(*shape):
    return pltpu.VMEM(shape, F32)


def near(values):
    return pltpu.with_memory_space_constraint(values, pltpu.VMEM)


def on_device(field, targets, weights):
    voxels = PLANES * ROWS * COLS * lax.axis_size(GY + GX)
    plane_count, line_count = lax.axis_size(PLANE), lax.axis_size(LINE)
    edge = resident(PLANES, OFFSETS, COLS)
    side = resident(128, COLS)
    vmem = pl.BlockSpec(memory_space=pltpu.VMEM)
    field = near(field)
    first, last = pl.pallas_call(
        columns_kernel,
        out_shape=(side, side),
        in_specs=[vmem],
        out_specs=(vmem,) * 2,
        name="columns",
    )(field)
    left = near(shift(last, GX, True))
    mine_near, mine_far = pl.pallas_call(
        rows_kernel, out_shape=(edge, edge), in_specs=[vmem] * 2, out_specs=(vmem,) * 2, name="rows"
    )(field, near(last))
    row_far = near(swap(mine_far, GY, 1))
    row_near = near(swap(mine_near, GY, 0))
    inner = pl.pallas_call(
        inner_kernel,
        out_shape=resident(1, 128),
        in_specs=[vmem],
        out_specs=vmem,
        name="inner",
        cost_estimate=pl.CostEstimate(flops=INNER, bytes_accessed=1 << 19, transcendentals=0),
    )(field)
    sums = pl.pallas_call(
        border_cols_kernel,
        out_shape=resident(1, 128),
        in_specs=[vmem] * 3,
        out_specs=vmem,
        name="border_cols",
        cost_estimate=pl.CostEstimate(flops=BORDER, bytes_accessed=1 << 17, transcendentals=0),
    )(left, near(first), near(inner))
    first_again = pl.pallas_call(
        again_kernel, out_shape=side, in_specs=[vmem] * 2, out_specs=vmem, name="again"
    )(near(first), near(sums))
    right = near(shift(first_again, GX, False))
    sums = pl.pallas_call(
        border_rows_kernel,
        out_shape=resident(plane_count, PAY, 128),
        in_specs=[vmem] * 5,
        out_specs=vmem,
        name="border_rows",
    )(near(mine_far), near(mine_near), row_far, row_near, near(sums))
    sums = pl.pallas_call(
        middle_kernel,
        out_shape=resident(line_count, 128),
        in_specs=[vmem],
        out_specs=vmem,
        name="middle",
    )(near(exchange(sums, PLANE)))
    totals = near(exchange(sums, LINE))
    settled = pl.pallas_call(
        settle_kernel, out_shape=resident(8, 128), in_specs=[vmem] * 2, out_specs=vmem, name="settle"
    )(right, near(sums))
    return pl.pallas_call(
        lambda *refs: gradient_kernel(voxels, *refs),
        out_shape=(jax.ShapeDtypeStruct((PLANES, ROWS, COLS), F32), jax.ShapeDtypeStruct((3, OFFSETS), F32)),
        in_specs=[vmem] * 9,
        out_specs=(HBM_SPEC, vmem),
        scratch_shapes=[
            pltpu.VMEM((PLANES, ROWS, COLS), F32),
            pltpu.SemaphoreType.DMA((GROUPS,)),
        ],
        name="gradient",
    )(field, row_far, row_near, left, right, totals, near(targets), near(weights), near(settled))


def solution(mesh):
    devices = np.asarray(mesh.devices).reshape(4, 4, 2, 4, 4)
    fine = Mesh(devices, GY + GX)
    return jax.shard_map(
        on_device,
        mesh=fine,
        in_specs=(P(None, GY, GX), P(), P()),
        out_specs=(P(None, GY, GX), P()),
        check_vma=False,
    )
```

time: 77.5 us -> 62.7 us (0.81)
  blocking collectives: 16.1 us -> 0 us
  starting transfers between devices: 38.8 us -> 42.9 us
  waiting for transfers between devices: 6.61 us -> 10.4 us
  Pallas kernels: 10.8 us -> 7.09 us
  local copies, waits for them, and re-layouts: 3.78 us -> 1.05 us
    all_to_all x1 -> x0, blocking collectives: 16.1 us -> none  [on_device(): sums = lax.all_to_all(sums, PLANE, 0, 0).sum(0)]
    ppermute x0 -> x2, starting transfers between devices: none -> 11 us  [swap(): lax.ppermute(block, axes, [pair for i, j in pairs for pair in ((i, j), (j...]
    ppermute x4 -> x2, starting transfers between devices: 28.4 us -> 17.8 us  [shift(): lax.ppermute(block, axes, [(i, (i + step) % count) for i in range(count)])]
    all_to_all x1 -> x2, waiting for transfers between devices: 0.01 us -> 10.4 us  [the longest x1 10.4 us: exchange(): return lax.all_to_all(parts[:, None], axes, 0, 0)[:, 0]]
    ppermute x4 -> x2, waiting for transfers between devices: 6.61 us -> 0.01 us  [shift(): lax.ppermute(block, axes, [(i, (i + step) % count) for i in range(count)])]
    pallas_call x4 -> x9, Pallas kernels: 10.8 us -> 7.09 us  [the longest x1 2.29 us: on_device(): pl.pallas_call(lambda *refs: gradient_kernel(voxels, *refs), out_shape=(j...]
    all_to_all x1 -> x2, starting transfers between devices: 10.5 us -> 14.1 us  [the longest x1 9.51 us: exchange(): return lax.all_to_all(parts[:, None], axes, 0, 0)[:, 0]]
    pad x2 -> x0, local copies, waits for them, and re-layouts: 1.18 us -> none  [the longest x1 0.6 us: on_device(): weights = jnp.pad(weights, ((0, 5), (0, 128 - OFFSETS)))]
  transfers between devices with their start and end apart: 5 -> 6, of which waited for: 2 -> 1; matrix products, arithmetic and copies ran while one was open for 2% -> 0% of each run, Pallas kernels for 4% -> 5%
where the time goes in v3:
time: 62.7 us; the launch traced here: 62.2 us
  starting transfers between devices  42.9 us (68%)
  waiting for transfers between devices  10.4 us (17%)
  Pallas kernels  7.09 us (11%)
  local copies, waits for them, and re-layouts  1.05 us (2%)
  between operations  0.76 us (1%)
    ppermute x2, starting transfers between devices, shift(): lax.ppermute(block, axes, [(i, (i + step) % count) for i in range(count)])  17.8 us
    ppermute x2, starting transfers between devices, swap(): lax.ppermute(block, axes, [pair for i, j in pairs for pair in ((i, j), (j...  11 us
    all_to_all x1, waiting for transfers between devices, exchange(): return lax.all_to_all(parts[:, None], axes, 0, 0)[:, 0]  10.4 us
    all_to_all x1, starting transfers between devices, exchange(): return lax.all_to_all(parts[:, None], axes, 0, 0)[:, 0]  9.51 us
    all_to_all x1, starting transfers between devices, exchange(): return lax.all_to_all(parts, axes, 0, 0)  4.58 us
    pallas_call x1, Pallas kernels, on_device(): pl.pallas_call(lambda *refs: gradient_kernel(voxels, *refs), out_shape=(j...  2.29 us
    pallas_call x1, Pallas kernels, on_device(): pl.pallas_call(inner_kernel, out_shape=resident(1, 128), in_specs=[vmem],...  1.37 us
    pallas_call x1, Pallas kernels, on_device(): pl.pallas_call(border_rows_kernel, out_shape=resident(plane_count, PAY, 1...  1.26 us
  transfers between devices with their start and end apart: 6, of which 1 were waited for; matrix products, arithmetic and copies ran while one was open for 0% of the time, Pallas kernels for 5%

profile of v3, /device:TPU:1, one launch (start us, length us, event | category | flops | bytes accessed | tf_op | source)
XLA Modules:
  0.0 62.2 jit_solution(15944032875971640725)
XLA Ops:
  0.6 0.0 copy-start
  0.6 1.0 %copy-done = f32[16,64,128]{2,1,0:T(8,128)S(1)} copy-done((f32[16,64,128]{2,1,0:T(8,128)S(1)}, f32[16,64,128]{2,1,0:T(8,128)}, u32[]{:S(2)}) %copy-start) | copy-done | bytes 524312
  1.7 0.2 columns.1
  1.9 9.6 %collective-permute-start.2 = (f32[128,128]{1,0:T(8,128)S(1)}, f32[128,128]{1,0:T(8,128)S(1)}, u32[]{:S(2)}, u32[]{:S(2)}) collective-permute-start(f32[128,128]{1,0:T(8,128)S(1)} %get-tuple-element.6.after), channel_id=1, source_target_pairs={{0,1},{1,2},{2,3},{3,4},{4,5},{5,6},{6,7},{7,8},{8,9},{9,10},{10,1... | collective-permute-start | bytes 196616 | tf_op jit(solution)/shard_map/ppermute | solution.py:251
  11.6 4.0 %collective-permute-start = (f32[16,16,128]{2,1,0:T(8,128)S(1)}, f32[16,16,128]{2,1,0:T(8,128)S(1)}, u32[]{:S(2)}, u32[]{:S(2)}) collective-permute-start(f32[16,16,128]{2,1,0:T(8,128)S(1)} %get-tuple-element.7.mine_far), channel_id=1, source_target_pairs={{16,32},{32,16},{48,64},{64,48},{80,96},{96,80},{112,128},{128,112... | collective-permute-start | bytes 393224 | tf_op jit(solution)/shard_map/ppermute | solution.py:257
  15.6 7.0 %collective-permute-start.1 = (f32[16,16,128]{2,1,0:T(8,128)S(1)}, f32[16,16,128]{2,1,0:T(8,128)S(1)}, u32[]{:S(2)}, u32[]{:S(2)}) collective-permute-start(f32[16,16,128]{2,1,0:T(8,128)S(1)} %get-tuple-element.8.mine_near), channel_id=1, source_target_pairs={{0,16},{16,0},{32,48},{48,32},{64,80},{80,64},{96,112},{112,96},{1... | collective-permute-start | bytes 393224 | tf_op jit(solution)/shard_map/ppermute | solution.py:257
  22.6 1.4 %inner.1 = f32[1,128]{1,0:T(1,128)S(1)} custom-call(f32[16,64,128]{2,1,0:T(8,128)S(1)} %copy-done), custom_call_target="tpu_custom_call" | custom-call | flops 600000000 | bytes 524288 | tf_op jit(solution)/shard_map/inner/pallas_call | solution.py:294
  24.0 0.0 collective-permute-done.2.left.refs_3_
  24.0 0.6 border_cols.1.after.sums
  24.5 0.0 collective-permute-done.row_far.refs_1_
  24.5 0.0 collective-permute-done.1.row_near.refs_2_
  24.6 1.3 %border_rows.1 = f32[32,8,128]{2,1,0:T(8,128)} custom-call(f32[16,16,128]{2,1,0:T(8,128)S(1)} %get-tuple-element.7.mine_far, f32[16,16,128]{2,1,0:T(8,128)S(1)} %get-tuple-element.8.mine_near, f32[16,16,128]{2,1,0:T(8,128)S(1)} %collective-permute-done.row_far.refs_1_, f32[16,16,128]{2,1,0:T(8,128)S(1)} %collective-permute-done.1.row_near.refs_2_, ...), custom_call_target="tpu_custom_call" | custom-call | tf_op jit(solution)/shard_map/border_rows/pallas_call | solution.py:314
  25.8 4.6 %all-to-all-start = ((f32[32,8,128]{2,1,0:T(8,128)}), f32[32,8,128]{2,1,0:T(8,128)S(1)}, u32[]{:S(2)}, u32[]{:S(2)}) async-start(f32[32,8,128]{2,1,0:T(8,128)} %border_rows.1), calls=%async_computation | async-start | bytes 262144 | tf_op jit(solution)/shard_map/all_to_all | solution.py:263
  30.4 8.2 %collective-permute-start.3 = (f32[128,128]{1,0:T(8,128)S(1)}, f32[128,128]{1,0:T(8,128)S(1)}, u32[]{:S(2)}, u32[]{:S(2)}) collective-permute-start(f32[128,128]{1,0:T(8,128)S(1)} %again.1), channel_id=1, source_target_pairs={{0,15},{1,0},{2,1},{3,2},{4,3},{5,4},{6,5},{7,6},{8,7},{9,8},{10,9... | collective-permute-start | bytes 196616 | tf_op jit(solution)/shard_map/ppermute | solution.py:251
  38.6 0.0 all-to-all-done.parts
  38.6 0.6 %middle.1.after = f32[16,128]{1,0:T(8,128)} custom-call(f32[32,8,128]{2,1,0:T(8,128)S(1)} %all-to-all-done.parts), custom_call_target="tpu_custom_call" | custom-call | tf_op jit(solution)/shard_map/middle/pallas_call | solution.py:321
  39.3 9.5 %all-to-all-start.1 = ((f32[16,1,128]{2,1,0:T(1,128)}), f32[16,1,128]{2,1,0:T(1,128)S(1)}, u32[]{:S(2)}, u32[]{:S(2)}) async-start(f32[16,1,128]{2,1,0:T(1,128)} %bitcast.1), calls=%async_computation.1 | async-start | bytes 16384 | tf_op jit(solution)/shard_map/all_to_all | solution.py:262
  48.8 0.0 collective-permute-done.3.right.refs_4_
  48.8 0.0 copy-start.2
  48.8 0.0 copy-start.3
  48.8 0.7 %settle.1.refs_8_ = f32[8,128]{1,0:T(8,128)S(1)} custom-call(f32[128,128]{1,0:T(8,128)S(1)} %collective-permute-done.3.right.refs_4_, f32[16,128]{1,0:T(8,128)} %middle.1.after), custom_call_target="tpu_custom_call" | custom-call | tf_op jit(solution)/shard_map/settle/pallas_call | solution.py:329
  49.5 10.4 %all-to-all-done.1 = f32[16,1,128]{2,1,0:T(1,128)S(1)} async-done(((f32[16,1,128]{2,1,0:T(1,128)}), f32[16,1,128]{2,1,0:T(1,128)S(1)}, u32[]{:S(2)}, u32[]{:S(2)}) %all-to-all-start.1) | async-done | bytes 8224 | tf_op jit(solution)/shard_map/all_to_all | solution.py:262
  59.9 0.0 copy-done.1
  60.0 2.3 %gradient.1 = (f32[16,64,128]{2,1,0:T(8,128)}, f32[3,16]{1,0:T(4,128)}) custom-call(f32[16,64,128]{2,1,0:T(8,128)S(1)} %copy-done.1, f32[16,16,128]{2,1,0:T(8,128)S(1)} %collective-permute-done.row_far.refs_1_, f32[16,16,128]{2,1,0:T(8,128)S(1)} %collective-permute-done.1.row_near.refs_2_, f32[128,128]{1,0:T(8,128)S(1)} %collective-permute-done.2.left.refs_3_, ...), custom_call_target="tpu_custom_call" | custom-call | tf_op jit(solution)/shard_map/gradient/pallas_call | solution.py:332
  (5 shorter events, 0.0 us)
Async XLA Ops:
  0.6 1.0 %copy-start = (f32[16,64,128]{2,1,0:T(8,128)S(1)}, f32[16,64,128]{2,1,0:T(8,128)}, u32[]{:S(2)}) copy-start(f32[16,64,128]{2,1,0:T(8,128)} %refs_0_.1) | copy-start | bytes 1572868
  1.9 22.1 %collective-permute-start.2 = (f32[128,128]{1,0:T(8,128)S(1)}, f32[128,128]{1,0:T(8,128)S(1)}, u32[]{:S(2)}, u32[]{:S(2)}) collective-permute-start(f32[128,128]{1,0:T(8,128)S(1)} %get-tuple-element.6.after), channel_id=1, source_target_pairs={{0,1},{1,2},{2,3},{3,4},{4,5},{5,6},{6,7},{7,8},{8,9},{9,10},{10,1... | collective-permute-start | bytes 196616 | tf_op jit(solution)/shard_map/ppermute | solution.py:251
  11.6 13.0 %collective-permute-start = (f32[16,16,128]{2,1,0:T(8,128)S(1)}, f32[16,16,128]{2,1,0:T(8,128)S(1)}, u32[]{:S(2)}, u32[]{:S(2)}) collective-permute-start(f32[16,16,128]{2,1,0:T(8,128)S(1)} %get-tuple-element.7.mine_far), channel_id=1, source_target_pairs={{16,32},{32,16},{48,64},{64,48},{80,96},{96,80},{112,128},{128,112... | collective-permute-start | bytes 393224 | tf_op jit(solution)/shard_map/ppermute | solution.py:257
  15.6 8.9 %collective-permute-start.1 = (f32[16,16,128]{2,1,0:T(8,128)S(1)}, f32[16,16,128]{2,1,0:T(8,128)S(1)}, u32[]{:S(2)}, u32[]{:S(2)}) collective-permute-start(f32[16,16,128]{2,1,0:T(8,128)S(1)} %get-tuple-element.8.mine_near), channel_id=1, source_target_pairs={{0,16},{16,0},{32,48},{48,32},{64,80},{80,64},{96,112},{112,96},{1... | collective-permute-start | bytes 393224 | tf_op jit(solution)/shard_map/ppermute | solution.py:257
  24.5 35.4 %copy-start.1 = (f32[16,64,128]{2,1,0:T(8,128)S(1)}, f32[16,64,128]{2,1,0:T(8,128)}, u32[]{:S(2)}) copy-start(f32[16,64,128]{2,1,0:T(8,128)} %refs_0_.1) | copy-start | bytes 1572868
  25.8 12.8 %all-to-all-start = ((f32[32,8,128]{2,1,0:T(8,128)}), f32[32,8,128]{2,1,0:T(8,128)S(1)}, u32[]{:S(2)}, u32[]{:S(2)}) async-start(f32[32,8,128]{2,1,0:T(8,128)} %border_rows.1), calls=%async_computation | async-start | bytes 262144 | tf_op jit(solution)/shard_map/all_to_all | solution.py:263
  30.4 18.4 %collective-permute-start.3 = (f32[128,128]{1,0:T(8,128)S(1)}, f32[128,128]{1,0:T(8,128)S(1)}, u32[]{:S(2)}, u32[]{:S(2)}) collective-permute-start(f32[128,128]{1,0:T(8,128)S(1)} %again.1), channel_id=1, source_target_pairs={{0,15},{1,0},{2,1},{3,2},{4,3},{5,4},{6,5},{7,6},{8,7},{9,8},{10,9... | collective-permute-start | bytes 196616 | tf_op jit(solution)/shard_map/ppermute | solution.py:251
  39.3 20.7 %all-to-all-start.1 = ((f32[16,1,128]{2,1,0:T(1,128)}), f32[16,1,128]{2,1,0:T(1,128)S(1)}, u32[]{:S(2)}, u32[]{:S(2)}) async-start(f32[16,1,128]{2,1,0:T(1,128)} %bitcast.1), calls=%async_computation.1 | async-start | bytes 16384 | tf_op jit(solution)/shard_map/all_to_all | solution.py:262
  48.8 11.2 %copy-start.2 = (f32[3,16]{1,0:T(4,128)S(1)}, f32[3,16]{1,0:T(4,128)}, u32[]{:S(2)}) copy-start(f32[3,16]{1,0:T(4,128)} %refs_6_.1) | copy-start | bytes 580
  48.8 11.1 %copy-start.3 = (f32[3,16]{1,0:T(4,128)S(1)}, f32[3,16]{1,0:T(4,128)}, u32[]{:S(2)}) copy-start(f32[3,16]{1,0:T(4,128)} %refs_7_.1) | copy-start | bytes 580

commit v4 on v3

--- a/solution.py
+++ b/solution.py
@@ -46,38 +46,38 @@
         values = gram[8 * block : 8 * block + 8]
         total = total + (pltpu.roll(values, by, 1) if by else values)
     row = iota((8, 128), 0)
-    for bit in (1, 2, 4):
-        total = jnp.where(row & bit != 0, pltpu.roll(total, 128 - bit, 1), total)
-    return jnp.sum(total, axis=0, keepdims=True)
-
-
-def one_row(*sums):
-    axis = iota((1, 128), 1) // OFFSETS
-    row = jnp.where(axis == 0, sums[0], 0.0)
-    for a in (1, 2):
-        row = jnp.where(axis == a, pltpu.roll(sums[a], OFFSETS * a, 1), row)
-    return row
-
-
-def columns_kernel(field, first, last):
+    moved = jnp.where(row == 0, total, 0.0)
+    for step in range(1, 8):
+        moved = jnp.where(row == step, pltpu.roll(total, 128 - step, 1), moved)
+    return jnp.sum(moved, axis=0, keepdims=True)
+
+
+def lanes(axis):
+    return OFFSETS * axis
+
+
+def only(axis, sums):
+    return jnp.where(iota((1, 128), 1) // OFFSETS == axis, sums, 0.0)
+
+
+def odd(axis):
+    return lax.axis_index(axis) % 2 == 1
+
+
+def swapped(flag, first, second):
+    return jnp.where(flag, second, first), jnp.where(flag, first, second)
+
+
+def columns_kernel(field, early, late):
     block = iota((128, COLS), 1) // OFFSETS
-    first_cols = jnp.zeros((128, COLS), F32)
-    last_cols = jnp.zeros((128, COLS), F32)
+    first = jnp.zeros((128, COLS), F32)
+    last = jnp.zeros((128, COLS), F32)
     for group in range(GROUPS):
         values = field[2 * group : 2 * group + 2].reshape(128, COLS)
         moved = pltpu.roll(values, OFFSETS * group, 1) if group else values
-        first_cols = jnp.where(block == group, moved, first_cols)
-        last_cols = jnp.where(block == (group + 7) % 8, moved, last_cols)
-    first[...] = first_cols
-    last[...] = last_cols
-
-
-def odd(axis):
-    return lax.axis_index(axis) % 2 == 1
-
-
-def swapped(flag, first, second):
-    return jnp.where(flag, second, first), jnp.where(flag, first, second)
+        first = jnp.where(block == group, moved, first)
+        last = jnp.where(block == (group + 7) % 8, moved, last)
+    early[...], late[...] = swapped(odd("c"), last, first)
 
 
 def rows_kernel(field, after, near_pair, far_pair):
@@ -86,12 +86,8 @@
     )
 
 
-def again_kernel(first, after, out):
-    out[...] = first[...]
-
-
-def settle_kernel(right, after, out):
-    out[...] = jnp.zeros_like(out)
+def again_kernel(late, after, out):
+    out[...] = late[...]
 
 
 def inner_kernel(field, out):
@@ -107,28 +103,30 @@
         both = jnp.concatenate(halves(field[plane]), axis=0)
         gram = gram + contract(both, both, ((1,), (1,)))
     apart = (col - row)[:ROWS]
-    along_rows = diagonal_sums(quadrants(gram), (apart >= 0) & (apart < OFFSETS) & (col[:ROWS] < ROWS), 0)
+    along_rows = diagonal_sums(
+        quadrants(gram), (apart >= 0) & (apart < OFFSETS) & (col[:ROWS] < ROWS), lanes(1)
+    )
     gram = jnp.zeros((256, 256), F32)
     for group in range(GROUPS):
         both = jnp.concatenate(halves(field[2 * group : 2 * group + 2].reshape(128, COLS)), axis=1)
         gram = gram + contract(both, both, ((0,), (0,)))
     apart = col - row
-    along_cols = diagonal_sums(quadrants(gram), (apart >= 0) & (apart < OFFSETS), 0)
+    along_cols = diagonal_sums(quadrants(gram), (apart >= 0) & (apart < OFFSETS), lanes(2))
     lane, offset = iota((OFFSETS, 128), 1), iota((OFFSETS, 128), 0)
     column = jnp.sum(jnp.where(lane == 8 * offset, spread, 0.0), axis=1, keepdims=True)
     along_planes = jnp.sum(jnp.where(lane == offset, column, 0.0), axis=0, keepdims=True)
-    out[...] = one_row(along_planes, along_rows, along_cols)
-
-
-def border_cols_kernel(left, first, inner, out):
+    out[...] = only(0, along_planes) + only(1, along_rows) + only(2, along_cols)
+
+
+def border_cols_kernel(received, late, inner, out):
+    left, right = swapped(odd("c"), received[...], late[...])
     row, col = iota((128, 128), 0), iota((128, 128), 1)
-    mine = jnp.concatenate(halves(left[...]), axis=1)
-    other = jnp.concatenate(halves(first[...]), axis=1)
+    mine = jnp.concatenate(halves(left), axis=1)
+    other = jnp.concatenate(halves(right), axis=1)
     gram = quadrants(contract(mine, other, ((0,), (0,))))
     apart = (col - row + 128) % 128
     keep = ((row // 16 + 1) % 8 == col // 16) & (apart < OFFSETS) & (apart > 0)
-    zeros = jnp.zeros((1, 128), F32)
-    out[...] = inner[...] + one_row(zeros, zeros, diagonal_sums(gram, keep, 0))
+    out[...] = inner[...] + only(2, diagonal_sums(gram, keep, lanes(2)))
 
 
 def border_rows_kernel(mine_far, mine_near, row_far, row_near, sums, out):
@@ -142,17 +140,18 @@
         product = contract(mine_high, jnp.concatenate([next_high, next_low], axis=0), ((1,), (1,)))
         gram = gram + product[:, :128] + product[:, 128:]
         gram = gram + contract(mine_low, next_high, ((1,), (1,)))
-    zeros = jnp.zeros((1, 128), F32)
-    along_rows = diagonal_sums(gram, (row // 16 == col // 16) & (col < row), OFFSETS)
-    out[...] = jnp.broadcast_to((sums[...] + one_row(zeros, along_rows, zeros))[None], out.shape)
+    along_rows = diagonal_sums(gram, (row // 16 == col // 16) & (col < row), OFFSETS + lanes(1))
+    out[...] = jnp.broadcast_to((sums[...] + only(1, along_rows))[None], out.shape)
 
 
 def gradient_kernel(
-    voxels, field, row_far, row_near, left, right, totals, targets, weights, after, gradient, correlation, result, sems
+    voxels, field, row_far, row_near, col_early, col_late, totals, targets, weights, gradient, correlation, result, value_ref, sems
 ):
     value = jnp.sum(totals[...], axis=0, keepdims=True) / jnp.float32(voxels)
     value = jnp.concatenate([value[:, OFFSETS * a : OFFSETS * (a + 1)] for a in range(3)], axis=0)
-    correlation[...] = value
+    value_ref[...] = value
+    copies = [pltpu.make_async_copy(value_ref, correlation, sems.at[GROUPS])]
+    copies[0].start()
     coefficient = weights[...] * (value - targets[...])
     lane, offset = iota((OFFSETS, 128), 1), iota((OFFSETS, 128), 0)
     same = iota((OFFSETS, OFFSETS), 0) == iota((OFFSETS, OFFSETS), 1)
@@ -201,6 +200,7 @@
         *halves(jnp.where(col == row, 2.0 * ahead, jnp.where(col > row, ahead, behind)))
     )
     below, above = swapped(odd("c"), row_near[...], row_far[...])
+    left, right = swapped(odd("c"), col_early[...], col_late[...])
 
     for pair in range(ROWS // 16):
         parts = []
@@ -215,10 +215,9 @@
 
     block = iota((128, COLS), 1) // OFFSETS
     col_right = jnp.concatenate([col_high, col_low], axis=1)
-    copies = []
     for group in range(GROUPS):
         values = field[2 * group : 2 * group + 2].reshape(128, COLS)
-        halo = jnp.where(block == group, right[...], left[...])
+        halo = jnp.where(block == group, right, left)
         if group:
             halo = pltpu.roll(halo, 128 - OFFSETS * group, 1)
         high, low = halves(jnp.concatenate([values, halo], axis=1))
@@ -245,10 +244,13 @@
     out[...] = jnp.broadcast_to(total, out.shape)
 
 
-def shift(block, axes, forward):
-    count = lax.axis_size(axes)
-    step = 1 if forward else count - 1
-    return lax.ppermute(block, axes, [(i, (i + step) % count) for i in range(count)])
+def pass_on(block, early):
+    rows, cols = lax.axis_size(GY), lax.axis_size(GX)
+    pairs = []
+    for row in range(rows):
+        step = 1 if (row % 2 == 0) == early else cols - 1
+        pairs += [(row * cols + i, row * cols + (i + step) % cols) for i in range(cols)]
+    return lax.ppermute(block, GY + GX, pairs)
 
 
 def swap(block, axes, shift):
@@ -278,17 +280,17 @@
     side = resident(128, COLS)
     vmem = pl.BlockSpec(memory_space=pltpu.VMEM)
     field = near(field)
-    first, last = pl.pallas_call(
+    early, late = pl.pallas_call(
         columns_kernel,
         out_shape=(side, side),
         in_specs=[vmem],
         out_specs=(vmem,) * 2,
         name="columns",
     )(field)
-    left = near(shift(last, GX, True))
+    col_early = near(pass_on(early, True))
     mine_near, mine_far = pl.pallas_call(
         rows_kernel, out_shape=(edge, edge), in_specs=[vmem] * 2, out_specs=(vmem,) * 2, name="rows"
-    )(field, near(last))
+    )(field, near(early))
     row_far = near(swap(mine_far, GY, 1))
     row_near = near(swap(mine_near, GY, 0))
     inner = pl.pallas_call(
@@ -306,11 +308,11 @@
         out_specs=vmem,
         name="border_cols",
         cost_estimate=pl.CostEstimate(flops=BORDER, bytes_accessed=1 << 17, transcendentals=0),
-    )(left, near(first), near(inner))
-    first_again = pl.pallas_call(
+    )(col_early, near(late), near(inner))
+    late_again = pl.pallas_call(
         again_kernel, out_shape=side, in_specs=[vmem] * 2, out_specs=vmem, name="again"
-    )(near(first), near(sums))
-    right = near(shift(first_again, GX, False))
+    )(near(late), near(sums))
+    col_late = near(pass_on(late_again, False))
     sums = pl.pallas_call(
         border_rows_kernel,
         out_shape=resident(plane_count, PAY, 128),
@@ -326,20 +328,18 @@
         name="middle",
     )(near(exchange(sums, PLANE)))
     totals = near(exchange(sums, LINE))
-    settled = pl.pallas_call(
-        settle_kernel, out_shape=resident(8, 128), in_specs=[vmem] * 2, out_specs=vmem, name="settle"
-    )(right, near(sums))
     return pl.pallas_call(
         lambda *refs: gradient_kernel(voxels, *refs),
         out_shape=(jax.ShapeDtypeStruct((PLANES, ROWS, COLS), F32), jax.ShapeDtypeStruct((3, OFFSETS), F32)),
-        in_specs=[vmem] * 9,
-        out_specs=(HBM_SPEC, vmem),
+        in_specs=[vmem] * 8,
+        out_specs=(HBM_SPEC, HBM_SPEC),
         scratch_shapes=[
             pltpu.VMEM((PLANES, ROWS, COLS), F32),
-            pltpu.SemaphoreType.DMA((GROUPS,)),
+            pltpu.VMEM((3, OFFSETS), F32),
+            pltpu.SemaphoreType.DMA((GROUPS + 1,)),
         ],
         name="gradient",
-    )(field, row_far, row_near, left, right, totals, near(targets), near(weights), near(settled))
+    )(field, row_far, row_near, col_early, col_late, totals, near(targets), near(weights))
 
 
 def solution(mesh):

time: 62.7 us -> 60.5 us (0.965)
  starting transfers between devices: 42.9 us -> 39.4 us
  waiting for transfers between devices: 10.4 us -> 13.7 us
  Pallas kernels: 7.09 us -> 5.2 us
    ppermute x2, starting transfers between devices: 11 us -> 8.31 us  [swap(): lax.ppermute(block, axes, [pair for i, j in pairs for pair in ((i, j), (j...]
    ppermute x2, starting transfers between devices: 17.8 us -> 20.5 us  [pass_on(): return lax.ppermute(block, GY + GX, pairs)]
    all_to_all x1, starting transfers between devices: 9.51 us -> 6.96 us  [exchange(): return lax.all_to_all(parts[:, None], axes, 0, 0)[:, 0]]
    all_to_all x1, waiting for transfers between devices: 0.01 us -> 2.51 us  [exchange(): return lax.all_to_all(parts, axes, 0, 0)]
    all_to_all x1, starting transfers between devices: 4.58 us -> 3.65 us  [exchange(): return lax.all_to_all(parts, axes, 0, 0)]
    all_to_all x1, waiting for transfers between devices: 10.4 us -> 11.1 us  [exchange(): return lax.all_to_all(parts[:, None], axes, 0, 0)[:, 0]]
    pallas_call x1 -> x0, Pallas kernels: 0.73 us -> none  [on_device(): pl.pallas_call(settle_kernel, out_shape=resident(8, 128), in_specs=[vmem]...]
  transfers between devices with their start and end apart: 6 -> 6, of which waited for: 1 -> 2; matrix products, arithmetic and copies ran while one was open for 0% -> 0% of each run, Pallas kernels for 5% -> 4%
where the time goes in v4:
time: 60.5 us; the launch traced here: 60.1 us
  starting transfers between devices  39.4 us (65%)
  waiting for transfers between devices  13.7 us (23%)
  Pallas kernels  5.2 us (9%)
  local copies, waits for them, and re-layouts  1.05 us (2%)
  between operations  0.77 us (1%)
    ppermute x2, starting transfers between devices, pass_on(): return lax.ppermute(block, GY + GX, pairs)  20.5 us
    all_to_all x1, waiting for transfers between devices, exchange(): return lax.all_to_all(parts[:, None], axes, 0, 0)[:, 0]  11.1 us
    ppermute x2, starting transfers between devices, swap(): lax.ppermute(block, axes, [pair for i, j in pairs for pair in ((i, j), (j...  8.31 us
    all_to_all x1, starting transfers between devices, exchange(): return lax.all_to_all(parts[:, None], axes, 0, 0)[:, 0]  6.96 us
    all_to_all x1, starting transfers between devices, exchange(): return lax.all_to_all(parts, axes, 0, 0)  3.65 us
    all_to_all x1, waiting for transfers between devices, exchange(): return lax.all_to_all(parts, axes, 0, 0)  2.51 us
    pallas_call x1, Pallas kernels, on_device(): pl.pallas_call(lambda *refs: gradient_kernel(voxels, *refs), out_shape=(j...  1.71 us
  transfers between devices with their start and end apart: 6, of which 2 were waited for; matrix products, arithmetic and copies ran while one was open for 0% of the time, Pallas kernels for 4%

profile of v4, /device:TPU:1, one launch (start us, length us, event | category | flops | bytes accessed | tf_op | source)
XLA Modules:
  0.0 60.1 jit_solution(9075355075247300520)
XLA Ops:
  0.6 0.0 copy-start
  0.6 1.0 %copy-done = f32[16,64,128]{2,1,0:T(8,128)S(1)} copy-done((f32[16,64,128]{2,1,0:T(8,128)S(1)}, f32[16,64,128]{2,1,0:T(8,128)}, u32[]{:S(2)}) %copy-start) | copy-done | bytes 524312
  1.7 0.2 columns.1
  1.9 15.5 %collective-permute-start.2 = (f32[128,128]{1,0:T(8,128)S(1)}, f32[128,128]{1,0:T(8,128)S(1)}, u32[]{:S(2)}, u32[]{:S(2)}) collective-permute-start(f32[128,128]{1,0:T(8,128)S(1)} %get-tuple-element.6.after), channel_id=1, source_target_pairs={{0,1},{1,2},{2,3},{3,4},{4,5},{5,6},{6,7},{7,8},{8,9},{9,10},{10,1... | collective-permute-start | bytes 196616 | tf_op jit(solution)/shard_map/ppermute | solution.py:253
  17.4 1.9 %collective-permute-start = (f32[16,16,128]{2,1,0:T(8,128)S(1)}, f32[16,16,128]{2,1,0:T(8,128)S(1)}, u32[]{:S(2)}, u32[]{:S(2)}) collective-permute-start(f32[16,16,128]{2,1,0:T(8,128)S(1)} %get-tuple-element.7.mine_far), channel_id=1, source_target_pairs={{16,32},{32,16},{48,64},{64,48},{80,96},{96,80},{112,128},{128,112... | collective-permute-start | bytes 393224 | tf_op jit(solution)/shard_map/ppermute | solution.py:259
  19.3 6.4 %collective-permute-start.1 = (f32[16,16,128]{2,1,0:T(8,128)S(1)}, f32[16,16,128]{2,1,0:T(8,128)S(1)}, u32[]{:S(2)}, u32[]{:S(2)}) collective-permute-start(f32[16,16,128]{2,1,0:T(8,128)S(1)} %get-tuple-element.8.mine_near), channel_id=1, source_target_pairs={{0,16},{16,0},{32,48},{48,32},{64,80},{80,64},{96,112},{112,96},{1... | collective-permute-start | bytes 393224 | tf_op jit(solution)/shard_map/ppermute | solution.py:259
  25.7 1.2 %inner.1 = f32[1,128]{1,0:T(1,128)S(1)} custom-call(f32[16,64,128]{2,1,0:T(8,128)S(1)} %copy-done), custom_call_target="tpu_custom_call" | custom-call | flops 600000000 | bytes 524288 | tf_op jit(solution)/shard_map/inner/pallas_call | solution.py:296
  26.9 0.0 collective-permute-done.2.received.refs_3_
  26.9 0.4 border_cols.1.after.sums
  27.3 0.0 copy-start.1
  27.3 0.0 collective-permute-done.row_far.refs_1_
  27.3 0.0 collective-permute-done.1.row_near.refs_2_
  27.3 1.1 %border_rows.1 = f32[32,8,128]{2,1,0:T(8,128)} custom-call(f32[16,16,128]{2,1,0:T(8,128)S(1)} %get-tuple-element.7.mine_far, f32[16,16,128]{2,1,0:T(8,128)S(1)} %get-tuple-element.8.mine_near, f32[16,16,128]{2,1,0:T(8,128)S(1)} %collective-permute-done.row_far.refs_1_, f32[16,16,128]{2,1,0:T(8,128)S(1)} %collective-permute-done.1.row_near.refs_2_, ...), custom_call_target="tpu_custom_call" | custom-call | tf_op jit(solution)/shard_map/border_rows/pallas_call | solution.py:316
  28.4 3.6 %all-to-all-start = ((f32[32,8,128]{2,1,0:T(8,128)}), f32[32,8,128]{2,1,0:T(8,128)S(1)}, u32[]{:S(2)}, u32[]{:S(2)}) async-start(f32[32,8,128]{2,1,0:T(8,128)} %border_rows.1), calls=%async_computation | async-start | bytes 262144 | tf_op jit(solution)/shard_map/all_to_all | solution.py:265
  32.1 5.0 %collective-permute-start.3 = (f32[128,128]{1,0:T(8,128)S(1)}, f32[128,128]{1,0:T(8,128)S(1)}, u32[]{:S(2)}, u32[]{:S(2)}) collective-permute-start(f32[128,128]{1,0:T(8,128)S(1)} %again.1), channel_id=1, source_target_pairs={{0,15},{1,0},{2,1},{3,2},{4,3},{5,4},{6,5},{7,6},{8,7},{9,8},{10,9... | collective-permute-start | bytes 196616 | tf_op jit(solution)/shard_map/ppermute | solution.py:253
  37.1 2.5 %all-to-all-done.parts = f32[32,8,128]{2,1,0:T(8,128)S(1)} async-done(((f32[32,8,128]{2,1,0:T(8,128)}), f32[32,8,128]{2,1,0:T(8,128)S(1)}, u32[]{:S(2)}, u32[]{:S(2)}) %all-to-all-start) | async-done | bytes 131104 | tf_op jit(solution)/shard_map/all_to_all | solution.py:265
  39.6 0.6 %middle.1 = f32[16,128]{1,0:T(8,128)} custom-call(f32[32,8,128]{2,1,0:T(8,128)S(1)} %all-to-all-done.parts), custom_call_target="tpu_custom_call" | custom-call | tf_op jit(solution)/shard_map/middle/pallas_call | solution.py:323
  40.2 7.0 %all-to-all-start.1 = ((f32[16,1,128]{2,1,0:T(1,128)}), f32[16,1,128]{2,1,0:T(1,128)S(1)}, u32[]{:S(2)}, u32[]{:S(2)}) async-start(f32[16,1,128]{2,1,0:T(1,128)} %bitcast.1), calls=%async_computation.1 | async-start | bytes 16384 | tf_op jit(solution)/shard_map/all_to_all | solution.py:264
  47.2 0.0 collective-permute-done.3.refs_4_
  47.2 11.1 %all-to-all-done.1 = f32[16,1,128]{2,1,0:T(1,128)S(1)} async-done(((f32[16,1,128]{2,1,0:T(1,128)}), f32[16,1,128]{2,1,0:T(1,128)S(1)}, u32[]{:S(2)}, u32[]{:S(2)}) %all-to-all-start.1) | async-done | bytes 8224 | tf_op jit(solution)/shard_map/all_to_all | solution.py:264
  58.4 0.0 copy-done.1
  58.4 0.0 copy-done.2
  58.4 0.0 copy-done.3
  58.4 1.7 %gradient.1 = (f32[16,64,128]{2,1,0:T(8,128)}, f32[3,16]{1,0:T(4,128)}) custom-call(f32[16,64,128]{2,1,0:T(8,128)S(1)} %copy-done.1, f32[16,16,128]{2,1,0:T(8,128)S(1)} %collective-permute-done.row_far.refs_1_, f32[16,16,128]{2,1,0:T(8,128)S(1)} %collective-permute-done.1.row_near.refs_2_, f32[128,128]{1,0:T(8,128)S(1)} %collective-permute-done.2.received.refs_3_, ...), custom_call_target="tpu_custom_call" | custom-call | tf_op jit(solution)/shard_map/gradient/pallas_call | solution.py:331
  (4 shorter events, 0.0 us)
Async XLA Ops:
  0.6 1.0 %copy-start = (f32[16,64,128]{2,1,0:T(8,128)S(1)}, f32[16,64,128]{2,1,0:T(8,128)}, u32[]{:S(2)}) copy-start(f32[16,64,128]{2,1,0:T(8,128)} %refs_0_.1) | copy-start | bytes 1572868
  1.9 25.1 %collective-permute-start.2 = (f32[128,128]{1,0:T(8,128)S(1)}, f32[128,128]{1,0:T(8,128)S(1)}, u32[]{:S(2)}, u32[]{:S(2)}) collective-permute-start(f32[128,128]{1,0:T(8,128)S(1)} %get-tuple-element.6.after), channel_id=1, source_target_pairs={{0,1},{1,2},{2,3},{3,4},{4,5},{5,6},{6,7},{7,8},{8,9},{9,10},{10,1... | collective-permute-start | bytes 196616 | tf_op jit(solution)/shard_map/ppermute | solution.py:253
  17.4 9.9 %collective-permute-start = (f32[16,16,128]{2,1,0:T(8,128)S(1)}, f32[16,16,128]{2,1,0:T(8,128)S(1)}, u32[]{:S(2)}, u32[]{:S(2)}) collective-permute-start(f32[16,16,128]{2,1,0:T(8,128)S(1)} %get-tuple-element.7.mine_far), channel_id=1, source_target_pairs={{16,32},{32,16},{48,64},{64,48},{80,96},{96,80},{112,128},{128,112... | collective-permute-start | bytes 393224 | tf_op jit(solution)/shard_map/ppermute | solution.py:259
  19.3 8.0 %collective-permute-start.1 = (f32[16,16,128]{2,1,0:T(8,128)S(1)}, f32[16,16,128]{2,1,0:T(8,128)S(1)}, u32[]{:S(2)}, u32[]{:S(2)}) collective-permute-start(f32[16,16,128]{2,1,0:T(8,128)S(1)} %get-tuple-element.8.mine_near), channel_id=1, source_target_pairs={{0,16},{16,0},{32,48},{48,32},{64,80},{80,64},{96,112},{112,96},{1... | collective-permute-start | bytes 393224 | tf_op jit(solution)/shard_map/ppermute | solution.py:259
  27.3 31.0 %copy-start.1 = (f32[16,64,128]{2,1,0:T(8,128)S(1)}, f32[16,64,128]{2,1,0:T(8,128)}, u32[]{:S(2)}) copy-start(f32[16,64,128]{2,1,0:T(8,128)} %refs_0_.1) | copy-start | bytes 1572868
  28.4 11.2 %all-to-all-start = ((f32[32,8,128]{2,1,0:T(8,128)}), f32[32,8,128]{2,1,0:T(8,128)S(1)}, u32[]{:S(2)}, u32[]{:S(2)}) async-start(f32[32,8,128]{2,1,0:T(8,128)} %border_rows.1), calls=%async_computation | async-start | bytes 262144 | tf_op jit(solution)/shard_map/all_to_all | solution.py:265
  32.1 15.1 %collective-permute-start.3 = (f32[128,128]{1,0:T(8,128)S(1)}, f32[128,128]{1,0:T(8,128)S(1)}, u32[]{:S(2)}, u32[]{:S(2)}) collective-permute-start(f32[128,128]{1,0:T(8,128)S(1)} %again.1), channel_id=1, source_target_pairs={{0,15},{1,0},{2,1},{3,2},{4,3},{5,4},{6,5},{7,6},{8,7},{9,8},{10,9... | collective-permute-start | bytes 196616 | tf_op jit(solution)/shard_map/ppermute | solution.py:253
  40.2 18.1 %copy-start.2 = (f32[3,16]{1,0:T(4,128)S(1)}, f32[3,16]{1,0:T(4,128)}, u32[]{:S(2)}) copy-start(f32[3,16]{1,0:T(4,128)} %refs_6_.1) | copy-start | bytes 580
  40.2 18.1 %copy-start.3 = (f32[3,16]{1,0:T(4,128)S(1)}, f32[3,16]{1,0:T(4,128)}, u32[]{:S(2)}) copy-start(f32[3,16]{1,0:T(4,128)} %refs_7_.1) | copy-start | bytes 580
  40.2 18.1 %all-to-all-start.1 = ((f32[16,1,128]{2,1,0:T(1,128)}), f32[16,1,128]{2,1,0:T(1,128)S(1)}, u32[]{:S(2)}, u32[]{:S(2)}) async-start(f32[16,1,128]{2,1,0:T(1,128)} %bitcast.1), calls=%async_computation.1 | async-start | bytes 16384 | tf_op jit(solution)/shard_map/all_to_all | solution.py:264

commit v5 on v4

--- a/solution.py
+++ b/solution.py
@@ -14,7 +14,8 @@
 PLANES, ROWS, COLS = 16, 64, 128
 GROUPS = 8
 F32, BF16 = jnp.float32, jnp.bfloat16
-PAY = 8
+PAY = 2
+MIDDLE = 300_000_000
 INNER, BORDER = 600_000_000, 2_000_000_000
 HBM_SPEC = pl.BlockSpec(memory_space=pl.ANY)
 
@@ -259,6 +260,10 @@
     return lax.ppermute(block, axes, [pair for i, j in pairs for pair in ((i, j), (j, i))])
 
 
+def settle_kernel(sums, after, out):
+    out[...] = sums[...]
+
+
 def exchange(parts, axes):
     if parts.ndim == 2:
         return lax.all_to_all(parts[:, None], axes, 0, 0)[:, 0]
@@ -315,19 +320,27 @@
     col_late = near(pass_on(late_again, False))
     sums = pl.pallas_call(
         border_rows_kernel,
-        out_shape=resident(plane_count, PAY, 128),
+        out_shape=resident(line_count, PAY, 128),
         in_specs=[vmem] * 5,
         out_specs=vmem,
         name="border_rows",
     )(near(mine_far), near(mine_near), row_far, row_near, near(sums))
     sums = pl.pallas_call(
         middle_kernel,
-        out_shape=resident(line_count, 128),
+        out_shape=resident(plane_count, 128),
         in_specs=[vmem],
         out_specs=vmem,
         name="middle",
-    )(near(exchange(sums, PLANE)))
-    totals = near(exchange(sums, LINE))
+        cost_estimate=pl.CostEstimate(flops=MIDDLE, bytes_accessed=1 << 14, transcendentals=0),
+    )(near(exchange(sums, LINE)))
+    sums = pl.pallas_call(
+        settle_kernel,
+        out_shape=resident(plane_count, 128),
+        in_specs=[vmem] * 2,
+        out_specs=vmem,
+        name="settle",
+    )(near(sums), col_late)
+    totals = near(exchange(sums, PLANE))
     return pl.pallas_call(
         lambda *refs: gradient_kernel(voxels, *refs),
         out_shape=(jax.ShapeDtypeStruct((PLANES, ROWS, COLS), F32), jax.ShapeDtypeStruct((3, OFFSETS), F32)),

time: 60.5 us -> 60.4 us (level)
  blocking collectives: 0 us -> 15 us
  waiting for transfers between devices: 13.7 us -> 4.18 us
  starting transfers between devices: 39.4 us -> 34.5 us
  Pallas kernels: 5.2 us -> 4.56 us
    all_to_all x0 -> x1, blocking collectives: none -> 15 us  [exchange(): return lax.all_to_all(parts[:, None], axes, 0, 0)[:, 0]]
    all_to_all x1 -> x0, waiting for transfers between devices: 11.1 us -> none  [exchange(): return lax.all_to_all(parts[:, None], axes, 0, 0)[:, 0]]
    all_to_all x1 -> x0, starting transfers between devices: 6.96 us -> none  [exchange(): return lax.all_to_all(parts[:, None], axes, 0, 0)[:, 0]]
    ppermute x2, starting transfers between devices: 20.5 us -> 22.7 us  [pass_on(): return lax.ppermute(block, GY + GX, pairs)]
    all_to_all x1, waiting for transfers between devices: 2.51 us -> 4 us  [exchange(): return lax.all_to_all(parts, axes, 0, 0)]
    pallas_call x2 -> x3, Pallas kernels: 1.7 us -> 1.04 us  [the longest x1 1.02 us: on_device(): pl.pallas_call(border_rows_kernel, out_shape=resident(line_count, PAY, 12...]
  transfers between devices with their start and end apart: 6 -> 5, of which waited for: 2 -> 2; matrix products, arithmetic and copies ran while one was open for 0% -> 0% of each run, Pallas kernels for 4% -> 3%
where the time goes in v5:
time: 60.4 us; the launch traced here: 60 us
  starting transfers between devices  34.5 us (57%)
  blocking collectives  15 us (25%)
  Pallas kernels  4.56 us (8%)
  waiting for transfers between devices  4.18 us (7%)
  local copies, waits for them, and re-layouts  1.05 us (2%)
  between operations  0.75 us (1%)
    ppermute x2, starting transfers between devices, pass_on(): return lax.ppermute(block, GY + GX, pairs)  22.7 us
    all_to_all x1, blocking collectives, exchange(): return lax.all_to_all(parts[:, None], axes, 0, 0)[:, 0]  15 us
    ppermute x2, starting transfers between devices, swap(): lax.ppermute(block, axes, [pair for i, j in pairs for pair in ((i, j), (j...  8.31 us
    all_to_all x1, waiting for transfers between devices, exchange(): return lax.all_to_all(parts, axes, 0, 0)  4 us
    all_to_all x1, starting transfers between devices, exchange(): return lax.all_to_all(parts, axes, 0, 0)  3.49 us
    pallas_call x1, Pallas kernels, on_device(): pl.pallas_call(lambda *refs: gradient_kernel(voxels, *refs), out_shape=(j...  1.72 us
  transfers between devices with their start and end apart: 5, of which 2 were waited for; matrix products, arithmetic and copies ran while one was open for 0% of the time, Pallas kernels for 3%

profile of v5, /device:TPU:1, one launch (start us, length us, event | category | flops | bytes accessed | tf_op | source)
XLA Modules:
  0.0 60.0 jit_solution(4777575040580945154)
XLA Ops:
  0.6 0.0 copy-start
  0.6 1.0 %copy-done = f32[16,64,128]{2,1,0:T(8,128)S(1)} copy-done((f32[16,64,128]{2,1,0:T(8,128)S(1)}, f32[16,64,128]{2,1,0:T(8,128)}, u32[]{:S(2)}) %copy-start) | copy-done | bytes 524312
  1.7 0.2 columns.1
  1.9 15.5 %collective-permute-start.2 = (f32[128,128]{1,0:T(8,128)S(1)}, f32[128,128]{1,0:T(8,128)S(1)}, u32[]{:S(2)}, u32[]{:S(2)}) collective-permute-start(f32[128,128]{1,0:T(8,128)S(1)} %get-tuple-element.6.after), channel_id=1, source_target_pairs={{0,1},{1,2},{2,3},{3,4},{4,5},{5,6},{6,7},{7,8},{8,9},{9,10},{10,1... | collective-permute-start | bytes 196616 | tf_op jit(solution)/shard_map/ppermute | solution.py:254
  17.4 1.9 %collective-permute-start = (f32[16,16,128]{2,1,0:T(8,128)S(1)}, f32[16,16,128]{2,1,0:T(8,128)S(1)}, u32[]{:S(2)}, u32[]{:S(2)}) collective-permute-start(f32[16,16,128]{2,1,0:T(8,128)S(1)} %get-tuple-element.7.mine_far), channel_id=1, source_target_pairs={{16,32},{32,16},{48,64},{64,48},{80,96},{96,80},{112,128},{128,112... | collective-permute-start | bytes 393224 | tf_op jit(solution)/shard_map/ppermute | solution.py:260
  19.3 6.4 %collective-permute-start.1 = (f32[16,16,128]{2,1,0:T(8,128)S(1)}, f32[16,16,128]{2,1,0:T(8,128)S(1)}, u32[]{:S(2)}, u32[]{:S(2)}) collective-permute-start(f32[16,16,128]{2,1,0:T(8,128)S(1)} %get-tuple-element.8.mine_near), channel_id=1, source_target_pairs={{0,16},{16,0},{32,48},{48,32},{64,80},{80,64},{96,112},{112,96},{1... | collective-permute-start | bytes 393224 | tf_op jit(solution)/shard_map/ppermute | solution.py:260
  25.7 1.2 %inner.1 = f32[1,128]{1,0:T(1,128)S(1)} custom-call(f32[16,64,128]{2,1,0:T(8,128)S(1)} %copy-done), custom_call_target="tpu_custom_call" | custom-call | flops 600000000 | bytes 524288 | tf_op jit(solution)/shard_map/inner/pallas_call | solution.py:301
  26.9 0.0 collective-permute-done.2.received.refs_3_
  26.9 0.4 border_cols.1.after.sums
  27.3 0.0 collective-permute-done.row_far.refs_1_
  27.3 0.0 collective-permute-done.1.row_near.refs_2_
  27.3 1.0 %border_rows.1 = f32[16,2,128]{2,1,0:T(2,128)} custom-call(f32[16,16,128]{2,1,0:T(8,128)S(1)} %get-tuple-element.7.mine_far, f32[16,16,128]{2,1,0:T(8,128)S(1)} %get-tuple-element.8.mine_near, f32[16,16,128]{2,1,0:T(8,128)S(1)} %collective-permute-done.row_far.refs_1_, f32[16,16,128]{2,1,0:T(8,128)S(1)} %collective-permute-done.1.row_near.refs_2_, ...), custom_call_target="tpu_custom_call" | custom-call | tf_op jit(solution)/shard_map/border_rows/pallas_call | solution.py:321
  28.4 3.5 %all-to-all-start = ((f32[16,2,128]{2,1,0:T(2,128)}), f32[16,2,128]{2,1,0:T(2,128)S(1)}, u32[]{:S(2)}, u32[]{:S(2)}) async-start(f32[16,2,128]{2,1,0:T(2,128)} %border_rows.1), calls=%async_computation | async-start | bytes 32768 | tf_op jit(solution)/shard_map/all_to_all | solution.py:270
  31.9 0.0 copy-start.1
  31.9 7.2 %collective-permute-start.3 = (f32[128,128]{1,0:T(8,128)S(1)}, f32[128,128]{1,0:T(8,128)S(1)}, u32[]{:S(2)}, u32[]{:S(2)}) collective-permute-start(f32[128,128]{1,0:T(8,128)S(1)} %again.1), channel_id=1, source_target_pairs={{0,15},{1,0},{2,1},{3,2},{4,3},{5,4},{6,5},{7,6},{8,7},{9,8},{10,9... | collective-permute-start | bytes 196616 | tf_op jit(solution)/shard_map/ppermute | solution.py:254
  39.1 4.0 %all-to-all-done.parts = f32[16,2,128]{2,1,0:T(2,128)S(1)} async-done(((f32[16,2,128]{2,1,0:T(2,128)}), f32[16,2,128]{2,1,0:T(2,128)S(1)}, u32[]{:S(2)}, u32[]{:S(2)}) %all-to-all-start) | async-done | bytes 16416 | tf_op jit(solution)/shard_map/all_to_all | solution.py:270
  43.1 0.2 collective-permute-done.3.after.refs_4_
  43.3 0.0 copy-start.2
  43.3 0.0 copy-start.3
  43.3 15.0 %all_to_all.10 = f32[32,1,128]{2,1,0:T(1,128)S(1)} all-to-all(f32[32,1,128]{2,1,0:T(1,128)S(1)} %bitcast.5), channel_id=1, replica_groups=mesh['zl'=4,'y'=4,'c'=2,'x'=4,'zh'=4] {'c','y','x'}, dimensions={0} | all-to-all | bytes 32768 | tf_op jit(solution)/shard_map/all_to_all | solution.py:269
  58.3 0.0 copy-done.1
  58.3 0.0 copy-done.2
  58.3 0.0 copy-done.3
  58.3 1.7 %gradient.1 = (f32[16,64,128]{2,1,0:T(8,128)}, f32[3,16]{1,0:T(4,128)}) custom-call(f32[16,64,128]{2,1,0:T(8,128)S(1)} %copy-done.1, f32[16,16,128]{2,1,0:T(8,128)S(1)} %collective-permute-done.row_far.refs_1_, f32[16,16,128]{2,1,0:T(8,128)S(1)} %collective-permute-done.1.row_near.refs_2_, f32[128,128]{1,0:T(8,128)S(1)} %collective-permute-done.2.received.refs_3_, ...), custom_call_target="tpu_custom_call" | custom-call | tf_op jit(solution)/shard_map/gradient/pallas_call | solution.py:344
  (4 shorter events, 0.1 us)
Async XLA Ops:
  0.6 1.0 %copy-start = (f32[16,64,128]{2,1,0:T(8,128)S(1)}, f32[16,64,128]{2,1,0:T(8,128)}, u32[]{:S(2)}) copy-start(f32[16,64,128]{2,1,0:T(8,128)} %refs_0_.1) | copy-start | bytes 1572868
  1.9 25.1 %collective-permute-start.2 = (f32[128,128]{1,0:T(8,128)S(1)}, f32[128,128]{1,0:T(8,128)S(1)}, u32[]{:S(2)}, u32[]{:S(2)}) collective-permute-start(f32[128,128]{1,0:T(8,128)S(1)} %get-tuple-element.6.after), channel_id=1, source_target_pairs={{0,1},{1,2},{2,3},{3,4},{4,5},{5,6},{6,7},{7,8},{8,9},{9,10},{10,1... | collective-permute-start | bytes 196616 | tf_op jit(solution)/shard_map/ppermute | solution.py:254
  17.4 9.9 %collective-permute-start = (f32[16,16,128]{2,1,0:T(8,128)S(1)}, f32[16,16,128]{2,1,0:T(8,128)S(1)}, u32[]{:S(2)}, u32[]{:S(2)}) collective-permute-start(f32[16,16,128]{2,1,0:T(8,128)S(1)} %get-tuple-element.7.mine_far), channel_id=1, source_target_pairs={{16,32},{32,16},{48,64},{64,48},{80,96},{96,80},{112,128},{128,112... | collective-permute-start | bytes 393224 | tf_op jit(solution)/shard_map/ppermute | solution.py:260
  19.3 8.0 %collective-permute-start.1 = (f32[16,16,128]{2,1,0:T(8,128)S(1)}, f32[16,16,128]{2,1,0:T(8,128)S(1)}, u32[]{:S(2)}, u32[]{:S(2)}) collective-permute-start(f32[16,16,128]{2,1,0:T(8,128)S(1)} %get-tuple-element.8.mine_near), channel_id=1, source_target_pairs={{0,16},{16,0},{32,48},{48,32},{64,80},{80,64},{96,112},{112,96},{1... | collective-permute-start | bytes 393224 | tf_op jit(solution)/shard_map/ppermute | solution.py:260
  28.4 14.7 %all-to-all-start = ((f32[16,2,128]{2,1,0:T(2,128)}), f32[16,2,128]{2,1,0:T(2,128)S(1)}, u32[]{:S(2)}, u32[]{:S(2)}) async-start(f32[16,2,128]{2,1,0:T(2,128)} %border_rows.1), calls=%async_computation | async-start | bytes 32768 | tf_op jit(solution)/shard_map/all_to_all | solution.py:270
  31.9 26.4 %copy-start.1 = (f32[16,64,128]{2,1,0:T(8,128)S(1)}, f32[16,64,128]{2,1,0:T(8,128)}, u32[]{:S(2)}) copy-start(f32[16,64,128]{2,1,0:T(8,128)} %refs_0_.1) | copy-start | bytes 1572868
  31.9 11.4 %collective-permute-start.3 = (f32[128,128]{1,0:T(8,128)S(1)}, f32[128,128]{1,0:T(8,128)S(1)}, u32[]{:S(2)}, u32[]{:S(2)}) collective-permute-start(f32[128,128]{1,0:T(8,128)S(1)} %again.1), channel_id=1, source_target_pairs={{0,15},{1,0},{2,1},{3,2},{4,3},{5,4},{6,5},{7,6},{8,7},{9,8},{10,9... | collective-permute-start | bytes 196616 | tf_op jit(solution)/shard_map/ppermute | solution.py:254
  43.3 15.0 %copy-start.2 = (f32[3,16]{1,0:T(4,128)S(1)}, f32[3,16]{1,0:T(4,128)}, u32[]{:S(2)}) copy-start(f32[3,16]{1,0:T(4,128)} %refs_6_.1) | copy-start | bytes 580
  43.3 15.0 %copy-start.3 = (f32[3,16]{1,0:T(4,128)S(1)}, f32[3,16]{1,0:T(4,128)}, u32[]{:S(2)}) copy-start(f32[3,16]{1,0:T(4,128)} %refs_7_.1) | copy-start | bytes 580

commit v6 on v4

--- a/solution.py
+++ b/solution.py
@@ -14,7 +14,8 @@
 PLANES, ROWS, COLS = 16, 64, 128
 GROUPS = 8
 F32, BF16 = jnp.float32, jnp.bfloat16
-PAY = 8
+PAY = 2
+MIDDLE = 300_000_000
 INNER, BORDER = 600_000_000, 2_000_000_000
 HBM_SPEC = pl.BlockSpec(memory_space=pl.ANY)
 
@@ -326,6 +327,7 @@
         in_specs=[vmem],
         out_specs=vmem,
         name="middle",
+        cost_estimate=pl.CostEstimate(flops=MIDDLE, bytes_accessed=1 << 14, transcendentals=0),
     )(near(exchange(sums, PLANE)))
     totals = near(exchange(sums, LINE))
     return pl.pallas_call(

time: 60.5 us -> 59.9 us (0.990)
  waiting for transfers between devices: 13.7 us -> 12.9 us
    all_to_all x1, waiting for transfers between devices: 2.51 us -> 1.78 us  [exchange(): return lax.all_to_all(parts, axes, 0, 0)]
where the time goes in v6:
time: 59.9 us; the launch traced here: 59.5 us
  starting transfers between devices  39.6 us (66%)
  waiting for transfers between devices  12.9 us (22%)
  Pallas kernels  5.17 us (9%)
  local copies, waits for them, and re-layouts  1.05 us (2%)
  between operations  0.77 us (1%)
    ppermute x2, starting transfers between devices, pass_on(): return lax.ppermute(block, GY + GX, pairs)  20.6 us
    all_to_all x1, waiting for transfers between devices, exchange(): return lax.all_to_all(parts[:, None], axes, 0, 0)[:, 0]  11.1 us
    ppermute x2, starting transfers between devices, swap(): lax.ppermute(block, axes, [pair for i, j in pairs for pair in ((i, j), (j...  8.31 us
    all_to_all x1, starting transfers between devices, exchange(): return lax.all_to_all(parts[:, None], axes, 0, 0)[:, 0]  6.99 us
    all_to_all x1, starting transfers between devices, exchange(): return lax.all_to_all(parts, axes, 0, 0)  3.64 us
    all_to_all x1, waiting for transfers between devices, exchange(): return lax.all_to_all(parts, axes, 0, 0)  1.78 us
    pallas_call x1, Pallas kernels, on_device(): pl.pallas_call(lambda *refs: gradient_kernel(voxels, *refs), out_shape=(j...  1.71 us
  transfers between devices with their start and end apart: 6, of which 2 were waited for; matrix products, arithmetic and copies ran while one was open for 0% of the time, Pallas kernels for 4%

profile of v6, /device:TPU:1, one launch (start us, length us, event | category | flops | bytes accessed | tf_op | source)
XLA Modules:
  0.0 59.5 jit_solution(3785227013348987931)
XLA Ops:
  0.6 0.0 copy-start
  0.6 1.0 %copy-done = f32[16,64,128]{2,1,0:T(8,128)S(1)} copy-done((f32[16,64,128]{2,1,0:T(8,128)S(1)}, f32[16,64,128]{2,1,0:T(8,128)}, u32[]{:S(2)}) %copy-start) | copy-done | bytes 524312
  1.7 0.2 columns.1
  1.9 15.5 %collective-permute-start.2 = (f32[128,128]{1,0:T(8,128)S(1)}, f32[128,128]{1,0:T(8,128)S(1)}, u32[]{:S(2)}, u32[]{:S(2)}) collective-permute-start(f32[128,128]{1,0:T(8,128)S(1)} %get-tuple-element.6.after), channel_id=1, source_target_pairs={{0,1},{1,2},{2,3},{3,4},{4,5},{5,6},{6,7},{7,8},{8,9},{9,10},{10,1... | collective-permute-start | bytes 196616 | tf_op jit(solution)/shard_map/ppermute | solution.py:254
  17.4 1.9 %collective-permute-start = (f32[16,16,128]{2,1,0:T(8,128)S(1)}, f32[16,16,128]{2,1,0:T(8,128)S(1)}, u32[]{:S(2)}, u32[]{:S(2)}) collective-permute-start(f32[16,16,128]{2,1,0:T(8,128)S(1)} %get-tuple-element.7.mine_far), channel_id=1, source_target_pairs={{16,32},{32,16},{48,64},{64,48},{80,96},{96,80},{112,128},{128,112... | collective-permute-start | bytes 393224 | tf_op jit(solution)/shard_map/ppermute | solution.py:260
  19.3 6.4 %collective-permute-start.1 = (f32[16,16,128]{2,1,0:T(8,128)S(1)}, f32[16,16,128]{2,1,0:T(8,128)S(1)}, u32[]{:S(2)}, u32[]{:S(2)}) collective-permute-start(f32[16,16,128]{2,1,0:T(8,128)S(1)} %get-tuple-element.8.mine_near), channel_id=1, source_target_pairs={{0,16},{16,0},{32,48},{48,32},{64,80},{80,64},{96,112},{112,96},{1... | collective-permute-start | bytes 393224 | tf_op jit(solution)/shard_map/ppermute | solution.py:260
  25.7 1.2 %inner.1 = f32[1,128]{1,0:T(1,128)S(1)} custom-call(f32[16,64,128]{2,1,0:T(8,128)S(1)} %copy-done), custom_call_target="tpu_custom_call" | custom-call | flops 600000000 | bytes 524288 | tf_op jit(solution)/shard_map/inner/pallas_call | solution.py:297
  26.9 0.0 collective-permute-done.2.received.refs_3_
  26.9 0.4 border_cols.1.after.sums
  27.3 0.0 collective-permute-done.row_far.refs_1_
  27.3 0.0 collective-permute-done.1.row_near.refs_2_
  27.3 1.0 %border_rows.1 = f32[32,2,128]{2,1,0:T(2,128)} custom-call(f32[16,16,128]{2,1,0:T(8,128)S(1)} %get-tuple-element.7.mine_far, f32[16,16,128]{2,1,0:T(8,128)S(1)} %get-tuple-element.8.mine_near, f32[16,16,128]{2,1,0:T(8,128)S(1)} %collective-permute-done.row_far.refs_1_, f32[16,16,128]{2,1,0:T(8,128)S(1)} %collective-permute-done.1.row_near.refs_2_, ...), custom_call_target="tpu_custom_call" | custom-call | tf_op jit(solution)/shard_map/border_rows/pallas_call | solution.py:317
  28.4 3.6 %all-to-all-start = ((f32[32,2,128]{2,1,0:T(2,128)}), f32[32,2,128]{2,1,0:T(2,128)S(1)}, u32[]{:S(2)}, u32[]{:S(2)}) async-start(f32[32,2,128]{2,1,0:T(2,128)} %border_rows.1), calls=%async_computation | async-start | bytes 65536 | tf_op jit(solution)/shard_map/all_to_all | solution.py:266
  32.0 0.0 copy-start.1
  32.0 5.1 %collective-permute-start.3 = (f32[128,128]{1,0:T(8,128)S(1)}, f32[128,128]{1,0:T(8,128)S(1)}, u32[]{:S(2)}, u32[]{:S(2)}) collective-permute-start(f32[128,128]{1,0:T(8,128)S(1)} %again.1), channel_id=1, source_target_pairs={{0,15},{1,0},{2,1},{3,2},{4,3},{5,4},{6,5},{7,6},{8,7},{9,8},{10,9... | collective-permute-start | bytes 196616 | tf_op jit(solution)/shard_map/ppermute | solution.py:254
  37.2 1.8 %all-to-all-done.parts = f32[32,2,128]{2,1,0:T(2,128)S(1)} async-done(((f32[32,2,128]{2,1,0:T(2,128)}), f32[32,2,128]{2,1,0:T(2,128)S(1)}, u32[]{:S(2)}, u32[]{:S(2)}) %all-to-all-start) | async-done | bytes 32800 | tf_op jit(solution)/shard_map/all_to_all | solution.py:266
  39.0 0.6 %middle.1 = f32[16,128]{1,0:T(8,128)} custom-call(f32[32,2,128]{2,1,0:T(2,128)S(1)} %all-to-all-done.parts), custom_call_target="tpu_custom_call" | custom-call | flops 300000000 | bytes 16384 | tf_op jit(solution)/shard_map/middle/pallas_call | solution.py:324
  39.6 7.0 %all-to-all-start.1 = ((f32[16,1,128]{2,1,0:T(1,128)}), f32[16,1,128]{2,1,0:T(1,128)S(1)}, u32[]{:S(2)}, u32[]{:S(2)}) async-start(f32[16,1,128]{2,1,0:T(1,128)} %bitcast.1), calls=%async_computation.1 | async-start | bytes 16384 | tf_op jit(solution)/shard_map/all_to_all | solution.py:265
  46.6 0.0 collective-permute-done.3.refs_4_
  46.6 11.1 %all-to-all-done.1 = f32[16,1,128]{2,1,0:T(1,128)S(1)} async-done(((f32[16,1,128]{2,1,0:T(1,128)}), f32[16,1,128]{2,1,0:T(1,128)S(1)}, u32[]{:S(2)}, u32[]{:S(2)}) %all-to-all-start.1) | async-done | bytes 8224 | tf_op jit(solution)/shard_map/all_to_all | solution.py:265
  57.8 0.0 copy-done.1
  57.8 0.0 copy-done.2
  57.8 0.0 copy-done.3
  57.8 1.7 %gradient.1 = (f32[16,64,128]{2,1,0:T(8,128)}, f32[3,16]{1,0:T(4,128)}) custom-call(f32[16,64,128]{2,1,0:T(8,128)S(1)} %copy-done.1, f32[16,16,128]{2,1,0:T(8,128)S(1)} %collective-permute-done.row_far.refs_1_, f32[16,16,128]{2,1,0:T(8,128)S(1)} %collective-permute-done.1.row_near.refs_2_, f32[128,128]{1,0:T(8,128)S(1)} %collective-permute-done.2.received.refs_3_, ...), custom_call_target="tpu_custom_call" | custom-call | tf_op jit(solution)/shard_map/gradient/pallas_call | solution.py:333
  (4 shorter events, 0.0 us)
Async XLA Ops:
  0.6 1.0 %copy-start = (f32[16,64,128]{2,1,0:T(8,128)S(1)}, f32[16,64,128]{2,1,0:T(8,128)}, u32[]{:S(2)}) copy-start(f32[16,64,128]{2,1,0:T(8,128)} %refs_0_.1) | copy-start | bytes 1572868
  1.9 25.1 %collective-permute-start.2 = (f32[128,128]{1,0:T(8,128)S(1)}, f32[128,128]{1,0:T(8,128)S(1)}, u32[]{:S(2)}, u32[]{:S(2)}) collective-permute-start(f32[128,128]{1,0:T(8,128)S(1)} %get-tuple-element.6.after), channel_id=1, source_target_pairs={{0,1},{1,2},{2,3},{3,4},{4,5},{5,6},{6,7},{7,8},{8,9},{9,10},{10,1... | collective-permute-start | bytes 196616 | tf_op jit(solution)/shard_map/ppermute | solution.py:254
  17.4 9.9 %collective-permute-start = (f32[16,16,128]{2,1,0:T(8,128)S(1)}, f32[16,16,128]{2,1,0:T(8,128)S(1)}, u32[]{:S(2)}, u32[]{:S(2)}) collective-permute-start(f32[16,16,128]{2,1,0:T(8,128)S(1)} %get-tuple-element.7.mine_far), channel_id=1, source_target_pairs={{16,32},{32,16},{48,64},{64,48},{80,96},{96,80},{112,128},{128,112... | collective-permute-start | bytes 393224 | tf_op jit(solution)/shard_map/ppermute | solution.py:260
  19.3 8.0 %collective-permute-start.1 = (f32[16,16,128]{2,1,0:T(8,128)S(1)}, f32[16,16,128]{2,1,0:T(8,128)S(1)}, u32[]{:S(2)}, u32[]{:S(2)}) collective-permute-start(f32[16,16,128]{2,1,0:T(8,128)S(1)} %get-tuple-element.8.mine_near), channel_id=1, source_target_pairs={{0,16},{16,0},{32,48},{48,32},{64,80},{80,64},{96,112},{112,96},{1... | collective-permute-start | bytes 393224 | tf_op jit(solution)/shard_map/ppermute | solution.py:260
  28.4 10.6 %all-to-all-start = ((f32[32,2,128]{2,1,0:T(2,128)}), f32[32,2,128]{2,1,0:T(2,128)S(1)}, u32[]{:S(2)}, u32[]{:S(2)}) async-start(f32[32,2,128]{2,1,0:T(2,128)} %border_rows.1), calls=%async_computation | async-start | bytes 65536 | tf_op jit(solution)/shard_map/all_to_all | solution.py:266
  32.0 25.7 %copy-start.1 = (f32[16,64,128]{2,1,0:T(8,128)S(1)}, f32[16,64,128]{2,1,0:T(8,128)}, u32[]{:S(2)}) copy-start(f32[16,64,128]{2,1,0:T(8,128)} %refs_0_.1) | copy-start | bytes 1572868
  32.0 14.6 %collective-permute-start.3 = (f32[128,128]{1,0:T(8,128)S(1)}, f32[128,128]{1,0:T(8,128)S(1)}, u32[]{:S(2)}, u32[]{:S(2)}) collective-permute-start(f32[128,128]{1,0:T(8,128)S(1)} %again.1), channel_id=1, source_target_pairs={{0,15},{1,0},{2,1},{3,2},{4,3},{5,4},{6,5},{7,6},{8,7},{9,8},{10,9... | collective-permute-start | bytes 196616 | tf_op jit(solution)/shard_map/ppermute | solution.py:254
  39.6 18.2 %copy-start.2 = (f32[3,16]{1,0:T(4,128)S(1)}, f32[3,16]{1,0:T(4,128)}, u32[]{:S(2)}) copy-start(f32[3,16]{1,0:T(4,128)} %refs_6_.1) | copy-start | bytes 580
  39.6 18.2 %copy-start.3 = (f32[3,16]{1,0:T(4,128)S(1)}, f32[3,16]{1,0:T(4,128)}, u32[]{:S(2)}) copy-start(f32[3,16]{1,0:T(4,128)} %refs_7_.1) | copy-start | bytes 580
  39.6 18.2 %all-to-all-start.1 = ((f32[16,1,128]{2,1,0:T(1,128)}), f32[16,1,128]{2,1,0:T(1,128)S(1)}, u32[]{:S(2)}, u32[]{:S(2)}) async-start(f32[16,1,128]{2,1,0:T(1,128)} %bitcast.1), calls=%async_computation.1 | async-start | bytes 16384 | tf_op jit(solution)/shard_map/all_to_all | solution.py:265

commit v7 on v6

--- a/solution.py
+++ b/solution.py
@@ -14,8 +14,7 @@
 PLANES, ROWS, COLS = 16, 64, 128
 GROUPS = 8
 F32, BF16 = jnp.float32, jnp.bfloat16
-PAY = 2
-MIDDLE = 300_000_000
+MIDDLE = 3_000_000_000
 INNER, BORDER = 600_000_000, 2_000_000_000
 HBM_SPEC = pl.BlockSpec(memory_space=pl.ANY)
 
@@ -142,7 +141,7 @@
         gram = gram + product[:, :128] + product[:, 128:]
         gram = gram + contract(mine_low, next_high, ((1,), (1,)))
     along_rows = diagonal_sums(gram, (row // 16 == col // 16) & (col < row), OFFSETS + lanes(1))
-    out[...] = jnp.broadcast_to((sums[...] + only(1, along_rows))[None], out.shape)
+    out[...] = jnp.broadcast_to(sums[...] + only(1, along_rows), out.shape)
 
 
 def gradient_kernel(
@@ -241,7 +240,7 @@
 
 
 def middle_kernel(parts, out):
-    total = jnp.sum(parts[...], axis=0)[:1]
+    total = jnp.sum(parts[...], axis=0, keepdims=True)
     out[...] = jnp.broadcast_to(total, out.shape)
 
 
@@ -316,7 +315,7 @@
     col_late = near(pass_on(late_again, False))
     sums = pl.pallas_call(
         border_rows_kernel,
-        out_shape=resident(plane_count, PAY, 128),
+        out_shape=resident(plane_count, 128),
         in_specs=[vmem] * 5,
         out_specs=vmem,
         name="border_rows",

time: 59.9 us -> 59.6 us (level)
    all_to_all x1 -> x2, starting transfers between devices: 6.99 us -> 10.7 us  [exchange(): return lax.all_to_all(parts[:, None], axes, 0, 0)[:, 0]]
    all_to_all x1 -> x0, starting transfers between devices: 3.64 us -> none  [exchange(): return lax.all_to_all(parts, axes, 0, 0)]
    all_to_all x1 -> x0, waiting for transfers between devices: 1.78 us -> none  [exchange(): return lax.all_to_all(parts, axes, 0, 0)]
    all_to_all x1 -> x2, waiting for transfers between devices: 11.1 us -> 12.8 us  [exchange(): return lax.all_to_all(parts[:, None], axes, 0, 0)[:, 0]]
where the time goes in v7:
time: 59.6 us; the launch traced here: 59.2 us
  starting transfers between devices  39.5 us (66%)
  waiting for transfers between devices  12.8 us (21%)
  Pallas kernels  5.12 us (9%)
  local copies, waits for them, and re-layouts  1.05 us (2%)
  between operations  0.76 us (1%)
    ppermute x2, starting transfers between devices, pass_on(): return lax.ppermute(block, GY + GX, pairs)  20.5 us
    all_to_all x2, waiting for transfers between devices, exchange(): return lax.all_to_all(parts[:, None], axes, 0, 0)[:, 0]  12.8 us
    all_to_all x2, starting transfers between devices, exchange(): return lax.all_to_all(parts[:, None], axes, 0, 0)[:, 0]  10.7 us
    ppermute x2, starting transfers between devices, swap(): lax.ppermute(block, axes, [pair for i, j in pairs for pair in ((i, j), (j...  8.31 us
    pallas_call x1, Pallas kernels, on_device(): pl.pallas_call(lambda *refs: gradient_kernel(voxels, *refs), out_shape=(j...  1.71 us
    pallas_call x1, Pallas kernels, on_device(): pl.pallas_call(inner_kernel, out_shape=resident(1, 128), in_specs=[vmem],...  1.19 us
  transfers between devices with their start and end apart: 6, of which 2 were waited for; matrix products, arithmetic and copies ran while one was open for 0% of the time, Pallas kernels for 4%

profile of v7, /device:TPU:1, one launch (start us, length us, event | category | flops | bytes accessed | tf_op | source)
XLA Modules:
  0.0 59.2 jit_solution(5853741706910081502)
XLA Ops:
  0.6 0.0 copy-start
  0.6 1.0 %copy-done = f32[16,64,128]{2,1,0:T(8,128)S(1)} copy-done((f32[16,64,128]{2,1,0:T(8,128)S(1)}, f32[16,64,128]{2,1,0:T(8,128)}, u32[]{:S(2)}) %copy-start) | copy-done | bytes 524312
  1.7 0.2 columns.1
  1.9 15.5 %collective-permute-start.2 = (f32[128,128]{1,0:T(8,128)S(1)}, f32[128,128]{1,0:T(8,128)S(1)}, u32[]{:S(2)}, u32[]{:S(2)}) collective-permute-start(f32[128,128]{1,0:T(8,128)S(1)} %get-tuple-element.6.after), channel_id=1, source_target_pairs={{0,1},{1,2},{2,3},{3,4},{4,5},{5,6},{6,7},{7,8},{8,9},{9,10},{10,1... | collective-permute-start | bytes 196616 | tf_op jit(solution)/shard_map/ppermute | solution.py:253
  17.4 1.9 %collective-permute-start = (f32[16,16,128]{2,1,0:T(8,128)S(1)}, f32[16,16,128]{2,1,0:T(8,128)S(1)}, u32[]{:S(2)}, u32[]{:S(2)}) collective-permute-start(f32[16,16,128]{2,1,0:T(8,128)S(1)} %get-tuple-element.7.mine_far), channel_id=1, source_target_pairs={{16,32},{32,16},{48,64},{64,48},{80,96},{96,80},{112,128},{128,112... | collective-permute-start | bytes 393224 | tf_op jit(solution)/shard_map/ppermute | solution.py:259
  19.3 6.4 %collective-permute-start.1 = (f32[16,16,128]{2,1,0:T(8,128)S(1)}, f32[16,16,128]{2,1,0:T(8,128)S(1)}, u32[]{:S(2)}, u32[]{:S(2)}) collective-permute-start(f32[16,16,128]{2,1,0:T(8,128)S(1)} %get-tuple-element.8.mine_near), channel_id=1, source_target_pairs={{0,16},{16,0},{32,48},{48,32},{64,80},{80,64},{96,112},{112,96},{1... | collective-permute-start | bytes 393224 | tf_op jit(solution)/shard_map/ppermute | solution.py:259
  25.7 1.2 %inner.1 = f32[1,128]{1,0:T(1,128)S(1)} custom-call(f32[16,64,128]{2,1,0:T(8,128)S(1)} %copy-done), custom_call_target="tpu_custom_call" | custom-call | flops 600000000 | bytes 524288 | tf_op jit(solution)/shard_map/inner/pallas_call | solution.py:296
  26.9 0.0 collective-permute-done.2.received.refs_3_
  26.9 0.4 border_cols.1.after.sums
  27.3 0.0 collective-permute-done.row_far.refs_1_
  27.3 0.0 collective-permute-done.1.row_near.refs_2_
  27.3 1.0 %border_rows.1 = f32[32,128]{1,0:T(8,128)} custom-call(f32[16,16,128]{2,1,0:T(8,128)S(1)} %get-tuple-element.7.mine_far, f32[16,16,128]{2,1,0:T(8,128)S(1)} %get-tuple-element.8.mine_near, f32[16,16,128]{2,1,0:T(8,128)S(1)} %collective-permute-done.row_far.refs_1_, f32[16,16,128]{2,1,0:T(8,128)S(1)} %collective-permute-done.1.row_near.refs_2_, ...), custom_call_target="tpu_custom_call" | custom-call | tf_op jit(solution)/shard_map/border_rows/pallas_call | solution.py:316
  28.3 3.6 %all-to-all-start = ((f32[32,1,128]{2,1,0:T(1,128)}), f32[32,1,128]{2,1,0:T(1,128)S(1)}, u32[]{:S(2)}, u32[]{:S(2)}) async-start(f32[32,1,128]{2,1,0:T(1,128)} %bitcast.1), calls=%async_computation | async-start | bytes 32768 | tf_op jit(solution)/shard_map/all_to_all | solution.py:264
  32.0 5.0 %collective-permute-start.3 = (f32[128,128]{1,0:T(8,128)S(1)}, f32[128,128]{1,0:T(8,128)S(1)}, u32[]{:S(2)}, u32[]{:S(2)}) collective-permute-start(f32[128,128]{1,0:T(8,128)S(1)} %again.1), channel_id=1, source_target_pairs={{0,15},{1,0},{2,1},{3,2},{4,3},{5,4},{6,5},{7,6},{8,7},{9,8},{10,9... | collective-permute-start | bytes 196616 | tf_op jit(solution)/shard_map/ppermute | solution.py:253
  37.0 1.7 %all-to-all-done = f32[32,1,128]{2,1,0:T(1,128)S(1)} async-done(((f32[32,1,128]{2,1,0:T(1,128)}), f32[32,1,128]{2,1,0:T(1,128)S(1)}, u32[]{:S(2)}, u32[]{:S(2)}) %all-to-all-start) | async-done | bytes 16416 | tf_op jit(solution)/shard_map/all_to_all | solution.py:264
  38.7 0.0 copy-start.1
  38.7 0.6 %middle.1 = f32[16,128]{1,0:T(8,128)} custom-call(f32[32,128]{1,0:T(8,128)S(1)} %bitcast.9), custom_call_target="tpu_custom_call" | custom-call | flops 3000000000 | bytes 16384 | tf_op jit(solution)/shard_map/middle/pallas_call | solution.py:323
  39.3 7.0 %all-to-all-start.1 = ((f32[16,1,128]{2,1,0:T(1,128)}), f32[16,1,128]{2,1,0:T(1,128)S(1)}, u32[]{:S(2)}, u32[]{:S(2)}) async-start(f32[16,1,128]{2,1,0:T(1,128)} %bitcast.4), calls=%async_computation.1 | async-start | bytes 16384 | tf_op jit(solution)/shard_map/all_to_all | solution.py:264
  46.4 0.0 collective-permute-done.3.refs_4_
  46.4 11.1 %all-to-all-done.1 = f32[16,1,128]{2,1,0:T(1,128)S(1)} async-done(((f32[16,1,128]{2,1,0:T(1,128)}), f32[16,1,128]{2,1,0:T(1,128)S(1)}, u32[]{:S(2)}, u32[]{:S(2)}) %all-to-all-start.1) | async-done | bytes 8224 | tf_op jit(solution)/shard_map/all_to_all | solution.py:264
  57.5 0.0 copy-done.1
  57.5 0.0 copy-done.2
  57.5 0.0 copy-done.3
  57.5 1.7 %gradient.1 = (f32[16,64,128]{2,1,0:T(8,128)}, f32[3,16]{1,0:T(4,128)}) custom-call(f32[16,64,128]{2,1,0:T(8,128)S(1)} %copy-done.1, f32[16,16,128]{2,1,0:T(8,128)S(1)} %collective-permute-done.row_far.refs_1_, f32[16,16,128]{2,1,0:T(8,128)S(1)} %collective-permute-done.1.row_near.refs_2_, f32[128,128]{1,0:T(8,128)S(1)} %collective-permute-done.2.received.refs_3_, ...), custom_call_target="tpu_custom_call" | custom-call | tf_op jit(solution)/shard_map/gradient/pallas_call | solution.py:332
  (4 shorter events, 0.0 us)
Async XLA Ops:
  0.6 1.0 %copy-start = (f32[16,64,128]{2,1,0:T(8,128)S(1)}, f32[16,64,128]{2,1,0:T(8,128)}, u32[]{:S(2)}) copy-start(f32[16,64,128]{2,1,0:T(8,128)} %refs_0_.1) | copy-start | bytes 1572868
  1.9 25.1 %collective-permute-start.2 = (f32[128,128]{1,0:T(8,128)S(1)}, f32[128,128]{1,0:T(8,128)S(1)}, u32[]{:S(2)}, u32[]{:S(2)}) collective-permute-start(f32[128,128]{1,0:T(8,128)S(1)} %get-tuple-element.6.after), channel_id=1, source_target_pairs={{0,1},{1,2},{2,3},{3,4},{4,5},{5,6},{6,7},{7,8},{8,9},{9,10},{10,1... | collective-permute-start | bytes 196616 | tf_op jit(solution)/shard_map/ppermute | solution.py:253
  17.4 9.9 %collective-permute-start = (f32[16,16,128]{2,1,0:T(8,128)S(1)}, f32[16,16,128]{2,1,0:T(8,128)S(1)}, u32[]{:S(2)}, u32[]{:S(2)}) collective-permute-start(f32[16,16,128]{2,1,0:T(8,128)S(1)} %get-tuple-element.7.mine_far), channel_id=1, source_target_pairs={{16,32},{32,16},{48,64},{64,48},{80,96},{96,80},{112,128},{128,112... | collective-permute-start | bytes 393224 | tf_op jit(solution)/shard_map/ppermute | solution.py:259
  19.3 8.0 %collective-permute-start.1 = (f32[16,16,128]{2,1,0:T(8,128)S(1)}, f32[16,16,128]{2,1,0:T(8,128)S(1)}, u32[]{:S(2)}, u32[]{:S(2)}) collective-permute-start(f32[16,16,128]{2,1,0:T(8,128)S(1)} %get-tuple-element.8.mine_near), channel_id=1, source_target_pairs={{0,16},{16,0},{32,48},{48,32},{64,80},{80,64},{96,112},{112,96},{1... | collective-permute-start | bytes 393224 | tf_op jit(solution)/shard_map/ppermute | solution.py:259
  28.3 10.3 %all-to-all-start = ((f32[32,1,128]{2,1,0:T(1,128)}), f32[32,1,128]{2,1,0:T(1,128)S(1)}, u32[]{:S(2)}, u32[]{:S(2)}) async-start(f32[32,1,128]{2,1,0:T(1,128)} %bitcast.1), calls=%async_computation | async-start | bytes 32768 | tf_op jit(solution)/shard_map/all_to_all | solution.py:264
  32.0 14.4 %collective-permute-start.3 = (f32[128,128]{1,0:T(8,128)S(1)}, f32[128,128]{1,0:T(8,128)S(1)}, u32[]{:S(2)}, u32[]{:S(2)}) collective-permute-start(f32[128,128]{1,0:T(8,128)S(1)} %again.1), channel_id=1, source_target_pairs={{0,15},{1,0},{2,1},{3,2},{4,3},{5,4},{6,5},{7,6},{8,7},{9,8},{10,9... | collective-permute-start | bytes 196616 | tf_op jit(solution)/shard_map/ppermute | solution.py:253
  38.7 18.8 %copy-start.1 = (f32[16,64,128]{2,1,0:T(8,128)S(1)}, f32[16,64,128]{2,1,0:T(8,128)}, u32[]{:S(2)}) copy-start(f32[16,64,128]{2,1,0:T(8,128)} %refs_0_.1) | copy-start | bytes 1572868
  39.3 18.2 %copy-start.2 = (f32[3,16]{1,0:T(4,128)S(1)}, f32[3,16]{1,0:T(4,128)}, u32[]{:S(2)}) copy-start(f32[3,16]{1,0:T(4,128)} %refs_6_.1) | copy-start | bytes 580
  39.3 18.2 %copy-start.3 = (f32[3,16]{1,0:T(4,128)S(1)}, f32[3,16]{1,0:T(4,128)}, u32[]{:S(2)}) copy-start(f32[3,16]{1,0:T(4,128)} %refs_7_.1) | copy-start | bytes 580
  39.3 18.2 %all-to-all-start.1 = ((f32[16,1,128]{2,1,0:T(1,128)}), f32[16,1,128]{2,1,0:T(1,128)S(1)}, u32[]{:S(2)}, u32[]{:S(2)}) async-start(f32[16,1,128]{2,1,0:T(1,128)} %bitcast.4), calls=%async_computation.1 | async-start | bytes 16384 | tf_op jit(solution)/shard_map/all_to_all | solution.py:264
